TPU v7x, 256 devices: a whole 4x4x8 slice. The times are simulated.
256 devices in a mesh: dp: 4 (over y_lo, core), row: 16 (over z, y_hi), col: 4 (over x).
Axes of the slice: x: 4, y: 4 (y_hi: 2, y_lo: 2; y = y_hi * 2 + y_lo), z: 8, core: 2. Of those that a mesh axis runs over, the one named last changes fastest.
Arguments:
- pair_act: bfloat16 [1024, 256, 128], P(('dp', 'row'), 'col'), parts along dimension 0, may hold values from -6 to 6
- gain_in: float32 [128], replicated, may hold values from 0.5 to 1.5
- bias_in: float32 [128], replicated, may hold values from -3 to 3
- proj_a: bfloat16 [1024, 256, 128], P(('dp', 'row'), 'col'), parts along dimension 0, may hold values from -6 to 6
- gate_a: bfloat16 [1024, 256, 128], P(('dp', 'row'), 'col'), parts along dimension 0, may hold values from -8 to 8
- proj_b: bfloat16 [1024, 256, 128], P(('dp', 'row'), 'col'), parts along dimension 0, may hold values from -6 to 6
- gate_b: bfloat16 [1024, 256, 128], P(('dp', 'row'), 'col'), parts along dimension 0, may hold values from -8 to 8
- tri_out: bfloat16 [1024, 256, 128], P(('dp', 'row'), 'col'), parts along dimension 0, may hold values from -12 to 12
- gain_tri: float32 [128], replicated, may hold values from 0.5 to 1.5
- bias_tri: float32 [128], replicated, may hold values from -3 to 3
- gate_out: bfloat16 [1024, 256, 128], P(('dp', 'row'), 'col'), parts along dimension 0, may hold values from -8 to 8
- cotangent: bfloat16 [1024, 256, 128], P(('dp', 'row'), 'col'), parts along dimension 0, may hold values from -6 to 6
- w_proj_a: bfloat16 [128, 128], replicated, may hold values from -0.5 to 0.5
- w_gate_a: bfloat16 [128, 128], replicated, may hold values from -0.5 to 0.5
- w_proj_b: bfloat16 [128, 128], replicated, may hold values from -0.5 to 0.5
- w_gate_b: bfloat16 [128, 128], replicated, may hold values from -0.5 to 0.5
- w_out: bfloat16 [128, 128], replicated, may hold values from -0.5 to 0.5
- w_gate: bfloat16 [128, 128], replicated, may hold values from -0.5 to 0.5
Outputs:
- pair_grad: bfloat16 [1024, 256, 128], P(('dp', 'row'), 'col'), parts along dimension 0
- gain_in_grad: float32 [512], P('dp'), parts along dimension 0
- bias_in_grad: float32 [512], P('dp'), parts along dimension 0
- gain_tri_grad: float32 [512], P('dp'), parts along dimension 0
- bias_tri_grad: float32 [512], P('dp'), parts along dimension 0
- w_proj_a_grad: float32 [512, 128], P('dp'), parts along dimension 0
- w_gate_a_grad: float32 [512, 128], P('dp'), parts along dimension 0
- w_proj_b_grad: float32 [512, 128], P('dp'), parts along dimension 0
- w_gate_b_grad: float32 [512, 128], P('dp'), parts along dimension 0
- w_out_grad: float32 [512, 128], P('dp'), parts along dimension 0
- w_gate_grad: float32 [512, 128], P('dp'), parts along dimension 0
There are 4 independent parts, one for each index of `dp`. A program takes and returns all parts, laid end to end along the dimension named above; an argument that names none is the same for every part. Nothing has to cross between parts.
All inputs are finite; a program needn't handle non-finite values.
Results may differ from a plain program's by a relative error of at most 0.0072.
Values may be sent and summed in bfloat16 or wider, within the bound.
A program may use at most 128 MiB of HBM per device.

v0:
```python
import jax
import jax.numpy as jnp
from jax import lax
from jax.sharding import PartitionSpec as P


def normalize(values):
    average = jnp.mean(values, axis=-1, keepdims=True)
    centred = values - average
    inverse = lax.rsqrt(jnp.mean(centred * centred, axis=-1, keepdims=True) + 1e-05)
    return (centred * inverse, inverse)


def norm_back(grad_hat, normed, inverse):
    grad_mean = jnp.mean(grad_hat, axis=-1, keepdims=True)
    grad_corr = jnp.mean(grad_hat * normed, axis=-1, keepdims=True)
    return inverse * (grad_hat - grad_mean - normed * grad_corr)


def outer_sum(left_mat, right_mat):
    return jnp.dot(left_mat.T, right_mat, preferred_element_type=jnp.float32)


def local(
    pair_act,
    gain_in,
    bias_in,
    proj_a,
    gate_a,
    proj_b,
    gate_b,
    tri_out,
    gain_tri,
    bias_tri,
    gate_out,
    cotangent,
    w_proj_a,
    w_gate_a,
    w_proj_b,
    w_gate_b,
    w_out,
    w_gate,
):
    rows_here, cols_here, feature = pair_act.shape
    hidden_w = tri_out.shape[2]
    normed, inverse = normalize(pair_act.astype(jnp.float32))
    pair_normed = (normed * gain_in + bias_in).astype(jnp.bfloat16)
    flat_normed = pair_normed.reshape(-1, feature)
    sig_a = jax.nn.sigmoid(gate_a.astype(jnp.float32))
    sig_b = jax.nn.sigmoid(gate_b.astype(jnp.float32))
    left_act = (sig_a * proj_a.astype(jnp.float32)).astype(jnp.bfloat16)
    right_act = (sig_b * proj_b.astype(jnp.float32)).astype(jnp.bfloat16)
    tri_hat, tri_inverse = normalize(tri_out.astype(jnp.float32))
    mixed_tri = (tri_hat * gain_tri + bias_tri).astype(jnp.bfloat16).reshape(-1, hidden_w)
    lifted = jnp.dot(mixed_tri, w_out, preferred_element_type=jnp.float32)
    sig_out = jax.nn.sigmoid(gate_out.astype(jnp.float32)).reshape(-1, feature)
    upstream = cotangent.astype(jnp.float32).reshape(-1, feature)
    grad_lift = (upstream * sig_out).astype(jnp.bfloat16)
    grad_gate = (upstream * lifted * sig_out * (1.0 - sig_out)).astype(jnp.bfloat16)
    grad_mixed = jnp.dot(grad_lift, w_out.T, preferred_element_type=jnp.float32)
    flat_hat = tri_hat.reshape(-1, hidden_w)
    out_terms = (
        outer_sum(mixed_tri, grad_lift),
        outer_sum(flat_normed, grad_gate),
        jnp.sum(grad_mixed * flat_hat, axis=0),
        jnp.sum(grad_mixed, axis=0),
    )
    out_terms = lax.psum((out_terms[0], out_terms[1], out_terms[2], out_terms[3]), ("row", "col"))
    grad_mixed = grad_mixed.reshape(rows_here, cols_here, hidden_w)
    grad_tri = norm_back(grad_mixed * gain_tri, tri_hat, tri_inverse).astype(jnp.bfloat16)
    tri_rows = lax.all_gather(grad_tri, "col", axis=1, tiled=True)
    tri_cols = lax.all_gather(grad_tri, "row", axis=0, tiled=True)
    row_index = lax.axis_index("row")
    full_grad = lax.all_gather(tri_cols, "col", axis=1, tiled=True)
    slab_grad = lax.dynamic_slice_in_dim(full_grad, row_index * rows_here, rows_here, 1)
    d_left = jnp.einsum(
        "ijc,jkc->ikc",
        tri_rows,
        lax.all_gather(right_act, "row", axis=0, tiled=True),
        preferred_element_type=jnp.float32,
    )
    d_right = jnp.einsum(
        "ijc,ikc->jkc",
        slab_grad,
        lax.all_gather(left_act, "row", axis=0, tiled=True),
        preferred_element_type=jnp.float32,
    )
    grad_pa = (d_left * sig_a).astype(jnp.bfloat16).reshape(-1, hidden_w)
    grad_ga = (
        (d_left * proj_a.astype(jnp.float32) * sig_a * (1.0 - sig_a))
        .astype(jnp.bfloat16)
        .reshape(-1, hidden_w)
    )
    grad_pb = (d_right * sig_b).astype(jnp.bfloat16).reshape(-1, hidden_w)
    grad_gb = (
        (d_right * proj_b.astype(jnp.float32) * sig_b * (1.0 - sig_b))
        .astype(jnp.bfloat16)
        .reshape(-1, hidden_w)
    )
    grad_normed = jnp.dot(grad_pa, w_proj_a.T, preferred_element_type=jnp.float32)
    grad_normed = grad_normed + jnp.dot(grad_ga, w_gate_a.T, preferred_element_type=jnp.float32)
    grad_normed = grad_normed + jnp.dot(grad_pb, w_proj_b.T, preferred_element_type=jnp.float32)
    grad_normed = grad_normed + jnp.dot(grad_gb, w_gate_b.T, preferred_element_type=jnp.float32)
    grad_normed = grad_normed + jnp.dot(grad_gate, w_gate.T, preferred_element_type=jnp.float32)
    flat_plain = normed.reshape(-1, feature)
    in_terms = (
        outer_sum(flat_normed, grad_pa),
        outer_sum(flat_normed, grad_ga),
        outer_sum(flat_normed, grad_pb),
        outer_sum(flat_normed, grad_gb),
        jnp.sum(grad_normed * flat_plain, axis=0),
        jnp.sum(grad_normed, axis=0),
    )
    in_terms = lax.psum(
        (in_terms[0], in_terms[1], in_terms[2], in_terms[3], in_terms[4], in_terms[5]),
        ("row", "col"),
    )
    grad_normed = grad_normed.reshape(rows_here, cols_here, feature)
    pair_grad = norm_back(grad_normed * gain_in, normed, inverse).astype(jnp.bfloat16)
    return (
        pair_grad,
        in_terms[4],
        in_terms[5],
        out_terms[2],
        out_terms[3],
        in_terms[0],
        in_terms[1],
        in_terms[2],
        in_terms[3],
        out_terms[0],
        out_terms[1],
    )


def solution(mesh):
    placed = (
        P(("dp", "row"), "col", None),
        P(),
        P(),
        P(("dp", "row"), "col", None),
        P(("dp", "row"), "col", None),
        P(("dp", "row"), "col", None),
        P(("dp", "row"), "col", None),
        P(("dp", "row"), "col", None),
        P(),
        P(),
        P(("dp", "row"), "col", None),
        P(("dp", "row"), "col", None),
        P(),
        P(),
        P(),
        P(),
        P(),
        P(),
    )
    return jax.shard_map(
        local,
        mesh=mesh,
        in_specs=placed,
        out_specs=(
            P(("dp", "row"), "col", None),
            P("dp"),
            P("dp"),
            P("dp"),
            P("dp"),
            P("dp", None),
            P("dp", None),
            P("dp", None),
            P("dp", None),
            P("dp", None),
            P("dp", None),
        ),
        check_vma=False,
    )
```

profile of v0, /device:TPU:8, one launch (start us, length us, event | category | flops | bytes accessed | tf_op | source)
XLA Modules:
  0.0 1396.3 jit_solution(15221859047536805567)
XLA Ops:
  7.2 0.0 all-gather.12.cloned.1.call-start
  7.2 1.1 add_divide_fusion.1
  8.3 1.2 convert_reduce_fusion
  9.5 1.3 fusion.7
  10.9 1.9 bitcast_subtract_fusion
  12.7 0.2 fusion.25
  13.0 1.5 add_convert_fusion.1
  14.5 1.4 fusion.23
  15.9 0.1 div.44
  16.0 2.3 multiply_convert_fusion.2
  18.3 0.0 all-gather.12.cloned.1.call-update
  18.3 0.0 all-gather.10.cloned.1.call-start
  18.3 1.9 fusion.16
  20.2 0.0 all-gather.10.cloned.1.call-update
  20.2 0.0 all-gather.14.cloned.1.call-start
  20.3 100.2 %all-gather.12.cloned.1.call-done = bf16[256,64,128]{2,1,0:T(8,128)(2,1)} async-done(((bf16[16,64,128]{2,1,0:T(8,128)(2,1)}), bf16[256,64,128]{2,1,0:T(8,128)(2,1)}) %all-gather.12.cloned.1.call-update) | async-done | bytes 4194320 | tf_op jit(solution)/shard_map/all_gather | solution.py:72
  120.5 6.8 copy.125
  127.3 0.0 all-gather.8.cloned.1.call-start
  127.4 0.9 copy.121
  128.2 0.0 all-gather.8.cloned.1.call-update
  128.3 0.0 all-gather.6.cloned.1.call-start
  128.3 91.3 %all-gather.10.cloned.1.call-done = bf16[256,64,128]{2,1,0:T(8,128)(2,1)} async-done(((bf16[16,64,128]{2,1,0:T(8,128)(2,1)}), bf16[256,64,128]{2,1,0:T(8,128)(2,1)}) %all-gather.10.cloned.1.call-update) | async-done | bytes 4194320 | tf_op jit(solution)/shard_map/all_gather | solution.py:85
  219.6 13.0 copy.127
  232.6 142.9 %all-gather.14.cloned.1.call-done = bf16[256,256,128]{2,0,1:T(8,128)(2,1)} async-done(((bf16[256,64,128]{2,0,1:T(8,128)(2,1)}), bf16[256,256,128]{2,0,1:T(8,128)(2,1)}) %all-gather.14.cloned.1.call-update) | async-done | bytes 16777232 | tf_op jit(solution)/shard_map/all_gather | solution.py:74
  375.5 1.3 constant_dynamic-slice_fusion
  376.8 0.9 copy.129
  377.7 4.6 fusion.29
  382.3 0.4 copy.128
  382.8 2.1 fusion.12
  384.8 0.0 all-gather.6.cloned.1.call-update
  384.9 0.2 all-reduce.4.cloned.1.call-start
  385.1 0.2 convert_reduce_fusion.1
  385.3 0.4 fusion.8
  385.7 1.9 convolution_bitcast_fusion
  387.6 1.4 fusion.2
  389.0 16.2 %all-gather.8.cloned.1.call-done = bf16[16,256,128]{2,0,1:T(8,128)(2,1)} async-done(((bf16[16,64,128]{2,0,1:T(8,128)(2,1)}), bf16[16,256,128]{2,0,1:T(8,128)(2,1)}) %all-gather.8.cloned.1.call-update) | async-done | bytes 1048592 | tf_op jit(solution)/shard_map/all_gather | solution.py:71
  405.2 2.2 copy.123
  407.4 99.8 %all-gather.6.cloned.1.call-done = bf16[256,64,128]{2,1,0:T(8,128)(2,1)} async-done(((bf16[16,64,128]{2,1,0:T(8,128)(2,1)}), bf16[256,64,128]{2,1,0:T(8,128)(2,1)}) %all-gather.6.cloned.1.call-update) | async-done | bytes 4194320 | tf_op jit(solution)/shard_map/all_gather | solution.py:79
  507.2 12.9 copy.122
  520.1 4.6 fusion.28
  524.7 0.4 copy.124
  525.2 1.2 fusion.15
  526.4 0.2 fusion.26
  526.6 0.2 convolution_add_fusion.3
  526.8 0.2 convolution_add_fusion.2
  527.1 1.0 convolution_add_fusion.1
  528.1 1.0 convolution_add_fusion
  529.1 1.2 add_convert_fusion
  530.2 0.9 convolution_bitcast_fusion.1
  531.1 0.9 convolution_bitcast_fusion.2
  532.0 0.9 convolution_bitcast_fusion.3
  532.9 0.9 convolution_bitcast_fusion.4
  533.8 0.9 fusion.27
  534.7 0.9 fusion.24
  535.6 0.1 div.48
  535.7 182.1 %all-reduce = (f32[128]{0:T(128)}, f32[128]{0:T(128)}, f32[128]{0:T(128)}, f32[128]{0:T(128)}) all-reduce(f32[128]{0:T(128)S(1)} %get-tuple-element.15, f32[128]{0:T(128)S(1)} %get-tuple-element.14, f32[128]{0:T(128)} %get-tuple-element.12, f32[128]{0:T(128)} %get-tuple-element.11), channel_id=1, replica_groups=mesh['dp'=4,'row'=16,'col'=4] {'row','col'}, use_global_device_ids=true, to_apply=%region_9.0 | all-reduce | flops 512 | bytes 4096 | tf_op jit(solution)/shard_map/psum | solution.py:114
  717.8 2.0 multiply_convert_fusion.1
  719.8 660.9 %all-reduce.4.cloned.1.call-done = (f32[128,128]{1,0:T(8,128)}, f32[128,128]{1,0:T(8,128)}, f32[128,128]{1,0:T(8,128)}, f32[128,128]{1,0:T(8,128)}, f32[128,128]{1,0:T(8,128)}, /*index=5*/f32[128,128]{1,0:T(8,128)}) async-done(((f32[128,128]{1,0:T(8,128)}, f32[128,128]{1,0:T(8,128)}, f32[128,128]{1,0:T(8,128)}, f32[128,128]{1,0:T(8,128)}, f32[128,128]{1,0:T(8,128)}, /*index=5*/f32[128,128]{1,0:T(8,128)}), ...) | async-done | bytes 393232 | tf_op jit(solution)/shard_map/psum | solution.py:114
  1380.6 1.5 copy.136
  1382.1 1.5 copy.137
  1383.6 1.5 copy.138
  1385.1 1.5 copy.139
  1386.5 1.5 copy.140
  1388.0 1.5 copy.141
  (28 shorter events, 0.1 us)
Async XLA Ops:
  7.2 5.6 copy-start
  7.2 113.3 %all-gather.12.cloned.1.call-start = ((), (), s32[]{:S(2)}) async-start(), calls=%async_computation.3 | async-start | bytes 4456448 | tf_op jit(solution)/shard_map/all_gather | solution.py:72
  14.5 371.2 %copy-start.5 = (bf16[16,64,128]{2,1,0:T(8,128)(2,1)}, bf16[16,64,128]{2,1,0:T(8,128)(2,1)S(1)}, u32[]{:S(2)}) copy-start(bf16[16,64,128]{2,1,0:T(8,128)(2,1)S(1)} %get-tuple-element.36) | copy-start | bytes 786436
  18.3 109.1 %copy-start.2 = (bf16[16,64,128]{2,1,0:T(8,128)(2,1)S(1)}, bf16[16,64,128]{2,1,0:T(8,128)(2,1)}, u32[]{:S(2)}) copy-start(bf16[16,64,128]{2,1,0:T(8,128)(2,1)} %multiply_convert_fusion.2) | copy-start | bytes 786436
  18.3 201.3 %all-gather.10.cloned.1.call-start = ((), (), s32[]{:S(2)}) async-start(), calls=%async_computation.2 | async-start | bytes 4456448 | tf_op jit(solution)/shard_map/all_gather | solution.py:85
  20.2 355.2 %all-gather.14.cloned.1.call-start = ((), (), s32[]{:S(2)}) async-start(), calls=%async_computation.4 | async-start | bytes 20971520 | tf_op jit(solution)/shard_map/all_gather | solution.py:74
  127.3 277.9 %all-gather.8.cloned.1.call-start = ((), (), s32[]{:S(2)}) async-start(), calls=%async_computation.1 | async-start | bytes 1310720 | tf_op jit(solution)/shard_map/all_gather | solution.py:71
  128.3 378.9 %all-gather.6.cloned.1.call-start = ((), (), s32[]{:S(2)}) async-start(), calls=%async_computation | async-start | bytes 4456448 | tf_op jit(solution)/shard_map/all_gather | solution.py:79
  377.7 7.4 copy-start.1
  377.7 8.0 copy-start.3
  384.9 995.8 %all-reduce.4.cloned.1.call-start = ((), (), s32[]{:S(2)}) async-start(), calls=%async_computation.5 | async-start | bytes 786432 | tf_op jit(solution)/shard_map/psum | solution.py:114
  520.1 5.1 copy-start.4
  520.1 6.3 copy-start.6
  520.1 6.5 copy-start.7
  520.1 6.8 copy-start.8
Sparse Core Ops, SparseCore 0:
  18.4 102.0 all-gather.11
  123.0 96.5 all-gather.9
  221.4 154.0 all-gather.13
  377.7 27.4 all-gather.7
  407.7 99.4 all-gather.5
  717.9 662.6 all-reduce.3
where the time goes:
time: 1400 us
  waiting for transfers between devices  1110 us (79%)
  blocking collectives  182 us (13%)
  local copies, waits for them, and re-layouts  47.8 us (3%)
  other arithmetic  20.4 us (1%)
  matrix products  19.9 us (1%)
  between operations  14.4 us (1%)
    psum x1, waiting for transfers between devices, local(): lax.psum((in_terms[0], in_terms[1], in_terms[2], in_terms[3], in_terms[4]...  661 us
    psum x1, blocking collectives, local(): lax.psum((in_terms[0], in_terms[1], in_terms[2], in_terms[3], in_terms[4]...  182 us
    all_gather x1, waiting for transfers between devices, local(): full_grad = lax.all_gather(tri_cols, 'col', axis=1, tiled=True)  143 us
    all_gather x1, waiting for transfers between devices, local(): tri_cols = lax.all_gather(grad_tri, 'row', axis=0, tiled=True)  100 us
    all_gather x1, waiting for transfers between devices, local(): lax.all_gather(right_act, 'row', axis=0, tiled=True)  99.8 us
    all_gather x1, waiting for transfers between devices, local(): lax.all_gather(left_act, 'row', axis=0, tiled=True)  91.3 us
  transfers between devices with their start and end apart: 6, of which 6 were waited for; matrix products, arithmetic and copies ran while one was open for 3% of the time, Pallas kernels for 0%

commit v1 on v0

v1 whole, which is shorter than its diff:
```python
import jax
import jax.numpy as jnp
from jax import lax
from jax.experimental import pallas as pl
from jax.experimental.pallas import tpu as pltpu
from jax.sharding import PartitionSpec as P

MESH = pl.DeviceIdType.MESH
F32 = jnp.float32
BF16 = jnp.bfloat16
ROWS = 16
COLS = 4
GROUP = ROWS * COLS
TI = 16
TJ = 64
CELLS = TI * TJ
CH = 128
STEP = 2
TURNS = TI // STEP
SPAN = STEP * TJ


def dot(a, b):
    return jnp.dot(a, b, preferred_element_type=F32)


def dot_nt(a, b):
    return lax.dot_general(a, b, (((1,), (1,)), ((), ())), preferred_element_type=F32)


def dot_tn(a, b):
    return lax.dot_general(a, b, (((0,), (0,)), ((), ())), preferred_element_type=F32)


def sigmoid(x):
    return 1.0 / (1.0 + jnp.exp(-x))


def normalize(values):
    average = jnp.mean(values, axis=-1, keepdims=True)
    centred = values - average
    inverse = lax.rsqrt(jnp.mean(centred * centred, axis=-1, keepdims=True) + 1e-05)
    return centred * inverse, inverse


def norm_back(grad_hat, normed, inverse):
    grad_mean = jnp.mean(grad_hat, axis=-1, keepdims=True)
    grad_corr = jnp.mean(grad_hat * normed, axis=-1, keepdims=True)
    return inverse * (grad_hat - grad_mean - normed * grad_corr)


def fold_rows(x):
    return jnp.sum(x.reshape(-1, 8, CH), axis=0)


def kernel(
    pair_act, proj_a, gate_a, proj_b, gate_b, tri_out, gate_out, cotangent,
    gain_in, bias_in, gain_tri, bias_tri,
    w_proj_a, w_gate_a, w_proj_b, w_gate_b, w_out, w_gate,
    pair_grad, vec_out, w_pa_g, w_ga_g, w_pb_g, w_gb_g, w_out_g, w_gate_g,
    tmp, tmp2, left_t, right_t, grad_t, left_r, right_r, grad_r,
    dl_s, dr_s, dl_r, dr_r, rbd,
    sig_a, sig_b, mixed_s, lift_s, ggate_s, normed_s, inv_s, pn_s, gn_s, ga1, ga2,
    part, part_r, total, final, vec_acc,
    send, recv,
):
    d, r, c = lax.axis_index("dp"), lax.axis_index("row"), lax.axis_index("col")
    mine = r * COLS + c

    def peer_of(k):
        return lax.rem(r + k // COLS, ROWS), lax.rem(c + lax.rem(k, COLS), COLS)

    barrier = pltpu.get_barrier_semaphore()

    def greet(k, _):
        pr, pc = peer_of(k)
        pl.semaphore_signal(barrier, inc=1, device_id=(d, pr, pc), device_id_type=MESH)
        return 0

    lax.fori_loop(1, GROUP, greet, 0)

    lane = lax.broadcasted_iota(jnp.int32, (TJ, CH), 1)
    low = lane < TJ
    row = lax.broadcasted_iota(jnp.int32, (TJ, CH), 0)
    fold = jnp.where(lax.rem(lane, TJ) == row, 1.0, 0.0).astype(BF16)

    def halves(x):
        zero = jnp.zeros_like(x)
        return jnp.concatenate([jnp.where(low, x, zero), jnp.where(low, zero, x)], axis=0)

    def turned(blocks):
        return dot_nt(fold, jnp.concatenate([halves(b) for b in blocks], axis=0).astype(BF16))

    def spread(scratch, s, flat):
        out = turned([flat[h * TJ : (h + 1) * TJ] for h in range(STEP)])
        for h in range(STEP):
            scratch[pl.ds(s * STEP + h, GROUP, stride=TI), :] = out[:, h * CH : (h + 1) * CH]

    def acts(s, _):
        at = pl.ds(s * STEP, STEP)
        for gate, proj, sig, scratch in ((gate_b, proj_b, sig_b, tmp), (gate_a, proj_a, sig_a, tmp2)):
            sg = sigmoid(gate[at].reshape(SPAN, CH).astype(F32))
            sig[pl.ds(s * SPAN, SPAN), :] = sg
            act = sg * proj[at].reshape(SPAN, CH).astype(F32)
            spread(scratch, s, act.astype(BF16).astype(F32))
        return 0

    lax.fori_loop(0, TURNS, acts, 0)
    right_t[...] = tmp[...].astype(BF16).reshape(GROUP, TI, CH)
    left_t[...] = tmp2[...].astype(BF16).reshape(GROUP, TI, CH)

    pl.semaphore_wait(barrier, GROUP - 1)

    def scatter(source, target, n):
        def go(k, _):
            pr, pc = peer_of(k)
            pltpu.make_async_remote_copy(
                src_ref=source.at[pr * COLS + pc], dst_ref=target.at[c, r],
                send_sem=send.at[n], recv_sem=recv.at[n],
                device_id=(d, pr, pc), device_id_type=MESH,
            ).start()
            return 0

        lax.fori_loop(1, GROUP, go, 0)
        target[c, r] = source[mine]

    def scatter_back(source, target, n):
        def go(k, _):
            pr, pc = peer_of(k)
            pltpu.make_async_remote_copy(
                src_ref=source.at[pc, pr], dst_ref=target.at[mine],
                send_sem=send.at[n], recv_sem=recv.at[n],
                device_id=(d, pr, pc), device_id_type=MESH,
            ).start()
            return 0

        lax.fori_loop(1, GROUP, go, 0)
        target[mine] = source[c, r]

    def arrived(n, like):
        view = like.at[pl.ds(0, GROUP - 1)]
        pltpu.make_async_copy(view, view, recv.at[n]).wait()

    def left_here(n, like):
        view = like.at[pl.ds(0, GROUP - 1)]
        pltpu.make_async_copy(view, view, send.at[n]).wait()

    scatter(right_t, right_r, 0)
    scatter(left_t, left_r, 1)

    g_tri, b_tri = gain_tri[...], bias_tri[...]
    vec_acc[...] = jnp.zeros_like(vec_acc)

    def outer(s, _):
        at, cells = pl.ds(s * STEP, STEP), pl.ds(s * SPAN, SPAN)
        hat, inv = normalize(tri_out[at].reshape(SPAN, CH).astype(F32))
        mixed = (hat * g_tri + b_tri).astype(BF16)
        lifted = dot(mixed, w_out[...])
        sg = sigmoid(gate_out[at].reshape(SPAN, CH).astype(F32))
        up = cotangent[at].reshape(SPAN, CH).astype(F32)
        ups = up * sg
        lift = ups.astype(BF16)
        ggate_s[cells, :] = (ups * lifted * (1.0 - sg)).astype(BF16)
        mixed_s[cells, :] = mixed
        lift_s[cells, :] = lift
        gm = dot_nt(lift, w_out[...])
        vec_acc[0] += fold_rows(gm * hat)
        vec_acc[1] += fold_rows(gm)
        gt = norm_back(gm * g_tri, hat, inv)
        spread(tmp, s, gt.astype(BF16).astype(F32))
        return 0

    lax.fori_loop(0, TURNS, outer, 0)
    grad_t[...] = tmp[...].astype(BF16).reshape(GROUP, TI, CH)
    scatter(grad_t, grad_r, 2)

    g_in, b_in = gain_in[...], bias_in[...]

    def first(s, _):
        at, cells = pl.ds(s * STEP, STEP), pl.ds(s * SPAN, SPAN)
        normed, inv = normalize(pair_act[at].reshape(SPAN, CH).astype(F32))
        normed_s[cells, :] = normed
        inv_s[cells, :] = jnp.broadcast_to(inv, (SPAN, CH))
        pn_s[cells, :] = (normed * g_in + b_in).astype(BF16)
        gn_s[cells, :] = dot_nt(ggate_s[cells, :], w_gate[...])
        return 0

    lax.fori_loop(0, TURNS, first, 0)
    part[:, 8:12, :] = jnp.concatenate(
        [dot_tn(mixed_s[...], lift_s[...]), dot_tn(pn_s[...], ggate_s[...])], axis=0
    ).reshape(GROUP, 4, CH)

    arrived(0, right_t)
    arrived(1, left_t)
    arrived(2, grad_t)
    for k in range(COLS):
        for j in range(COLS):
            tile = right_r[k, 4 * j : 4 * j + 4].reshape(TJ, CH)
            rbd[j * CH : (j + 1) * CH, k * CH : (k + 1) * CH] = halves(tile.astype(F32)).astype(BF16)
    grads = jnp.concatenate([grad_r[k].reshape(ROWS * TI, CH) for k in range(COLS)], axis=1)
    lefts = jnp.concatenate([left_r[k].reshape(ROWS * TI, CH) for k in range(COLS)], axis=1)
    d_left = dot(grads, rbd[...]).astype(BF16)
    for k in range(COLS):
        dl_s[k] = d_left[:, k * CH : (k + 1) * CH].reshape(ROWS, TI, CH)
    scatter_back(dl_s, dl_r, 3)
    d_right = dot_tn(grads, lefts)
    for k in range(COLS):
        for j in range(COLS):
            tile = d_right[j * CH : (j + 1) * CH, k * CH : (k + 1) * CH]
            dr_s[k, 4 * j : 4 * j + 4] = (
                jnp.where(low, tile[:TJ], tile[TJ:]).astype(BF16).reshape(4, TI, CH)
            )
    scatter_back(dr_s, dr_r, 4)

    def side(arr, n, like, sig, proj, wp, wg, base):
        arrived(n, like)
        tmp[...] = arr[...].reshape(CELLS, CH).astype(F32)

        def go(s, _):
            at, cells = pl.ds(s * STEP, STEP), pl.ds(s * SPAN, SPAN)
            blocks = [tmp[pl.ds(s * STEP + h, GROUP, stride=TI), :] for h in range(STEP)]
            out = turned(blocks)
            dd = jnp.concatenate([out[:, h * CH : (h + 1) * CH] for h in range(STEP)], axis=0)
            sg = sig[cells, :]
            ds = dd * sg
            gp = ds.astype(BF16)
            gg = (ds * proj[at].reshape(SPAN, CH).astype(F32) * (1.0 - sg)).astype(BF16)
            ga1[cells, :] = gp
            ga2[cells, :] = gg
            gn_s[cells, :] += dot_nt(gp, wp[...]) + dot_nt(gg, wg[...])
            return 0

        lax.fori_loop(0, TURNS, go, 0)
        part[base : base + 16, 0:8, :] = dot_tn(pn_s[...], ga1[...]).reshape(16, 8, CH)
        part[base + 16 : base + 32, 0:8, :] = dot_tn(pn_s[...], ga2[...]).reshape(16, 8, CH)

    side(dl_r, 3, dl_s_like(right_t), sig_a, proj_a, w_proj_a, w_gate_a, 0)
    side(dr_r, 4, dl_s_like(right_t), sig_b, proj_b, w_proj_b, w_gate_b, 32)

    def last(s, _):
        at, cells = pl.ds(s * STEP, STEP), pl.ds(s * SPAN, SPAN)
        gn, normed = gn_s[cells, :], normed_s[cells, :]
        vec_acc[2] += fold_rows(gn * normed)
        vec_acc[3] += fold_rows(gn)
        back = norm_back(gn * g_in, normed, inv_s[cells, :])
        pair_grad[at] = back.astype(BF16).reshape(STEP, TJ, CH)
        return 0

    lax.fori_loop(0, TURNS, last, 0)
    vecs = jnp.concatenate([jnp.sum(vec_acc[n], axis=0, keepdims=True) for n in range(4)], axis=0)
    part[:, 12:16, :] = jnp.broadcast_to(vecs[None], (GROUP, 4, CH))

    def reduce_go(k, _):
        pr, pc = peer_of(k)
        pltpu.make_async_remote_copy(
            src_ref=part.at[pr * COLS + pc], dst_ref=part_r.at[mine],
            send_sem=send.at[5], recv_sem=recv.at[5],
            device_id=(d, pr, pc), device_id_type=MESH,
        ).start()
        return 0

    lax.fori_loop(1, GROUP, reduce_go, 0)
    part_r[mine] = part[mine]
    arrived(5, part)
    total[...] = jnp.sum(part_r[...], axis=0)

    def gather_go(k, _):
        pr, pc = peer_of(k)
        pltpu.make_async_remote_copy(
            src_ref=total, dst_ref=final.at[mine],
            send_sem=send.at[6], recv_sem=recv.at[6],
            device_id=(d, pr, pc), device_id_type=MESH,
        ).start()
        return 0

    lax.fori_loop(1, GROUP, gather_go, 0)
    final[mine] = total[...]
    vec_out[...] = total[12:16, :]
    arrived(6, part)
    for n, ref in enumerate((w_pa_g, w_ga_g, w_pb_g, w_gb_g)):
        ref[...] = final[16 * n : 16 * n + 16, 0:8, :].reshape(CH, CH)
    both = final[:, 8:12, :].reshape(2 * CH, CH)
    w_out_g[...] = both[:CH]
    w_gate_g[...] = both[CH:]
    for n in range(5):
        left_here(n, right_t)
    left_here(5, part)
    left_here(6, part)


def dl_s_like(ref):
    return ref


def local(
    pair_act, gain_in, bias_in, proj_a, gate_a, proj_b, gate_b, tri_out, gain_tri, bias_tri,
    gate_out, cotangent, w_proj_a, w_gate_a, w_proj_b, w_gate_b, w_out, w_gate,
):
    vmem = pl.BlockSpec(memory_space=pltpu.VMEM)
    square = jax.ShapeDtypeStruct((CH, CH), F32)
    turned = pltpu.VMEM((GROUP, TI, CH), BF16)
    landed = pltpu.VMEM((COLS, ROWS, TI, CH), BF16)
    wide = pltpu.VMEM((CELLS, CH), F32)
    half = pltpu.VMEM((CELLS, CH), BF16)
    outs = pl.pallas_call(
        kernel,
        out_shape=(
            jax.ShapeDtypeStruct(pair_act.shape, BF16),
            jax.ShapeDtypeStruct((4, CH), F32),
            square, square, square, square, square, square,
        ),
        in_specs=[vmem] * 18,
        out_specs=tuple([vmem] * 8),
        scratch_shapes=[
            wide, wide, turned, turned, turned, landed, landed, landed,
            landed, landed, turned, turned, pltpu.VMEM((4 * CH, 4 * CH), BF16),
            wide, wide, half, half, half, wide, wide, half, wide, half, half,
            pltpu.VMEM((GROUP, 16, CH), F32), pltpu.VMEM((GROUP, 16, CH), F32),
            pltpu.VMEM((16, CH), F32), pltpu.VMEM((GROUP, 16, CH), F32), pltpu.VMEM((4, 8, CH), F32),
            pltpu.SemaphoreType.DMA((7,)), pltpu.SemaphoreType.DMA((7,)),
        ],
        compiler_params=pltpu.CompilerParams(
            collective_id=0, has_side_effects=True, vmem_limit_bytes=48 * 1024 * 1024
        ),
        name="triangle_backward",
    )(
        pair_act, proj_a, gate_a, proj_b, gate_b, tri_out, gate_out, cotangent,
        gain_in.reshape(1, CH), bias_in.reshape(1, CH), gain_tri.reshape(1, CH), bias_tri.reshape(1, CH),
        w_proj_a, w_gate_a, w_proj_b, w_gate_b, w_out, w_gate,
    )
    pair_grad, vecs, w_pa, w_ga, w_pb, w_gb, w_o, w_g = outs
    return (pair_grad, vecs[2], vecs[3], vecs[0], vecs[1], w_pa, w_ga, w_pb, w_gb, w_o, w_g)


def solution(mesh):
    tile = P(("dp", "row"), "col", None)
    placed = (
        tile, P(), P(), tile, tile, tile, tile, tile, P(), P(),
        tile, tile, P(), P(), P(), P(), P(), P(),
    )
    vector, matrix = P("dp"), P("dp", None)
    return jax.shard_map(
        local,
        mesh=mesh,
        in_specs=placed,
        out_specs=(tile,) + (vector,) * 4 + (matrix,) * 6,
        check_vma=False,
    )
```

time: 1400 us -> 104 us (0.07)
  the two profiles are of different devices: /device:TPU:8 before, /device:TPU:64 now
where the time goes in v1:
time: 104 us; the launch traced here: 103 us
  Pallas kernels  84.7 us (81%)
  local copies, waits for them, and re-layouts  17.8 us (17%)
    pallas_call x1, Pallas kernels, local(): pl.pallas_call(kernel, out_shape=(jax.ShapeDtypeStruct(pair_act.shape, BF...  84.7 us
    unnamed x43, local copies, waits for them, and re-layouts  17.3 us

profile of v1, /device:TPU:64, one launch (start us, length us, event | category | flops | bytes accessed | tf_op | source)
XLA Modules:
  0.0 103.3 jit_solution(5100461355640742492)
XLA Ops:
  0.7 0.0 copy-start.17
  0.7 0.0 copy-start.14
  0.7 0.0 copy-start.15
  0.7 0.0 copy-start.16
  0.7 0.6 copy-done.17
  1.3 0.0 copy-done.14
  1.3 0.0 copy-done.15
  1.3 0.0 copy-done.16
  1.4 0.0 copy-start
  1.4 0.9 copy-done
  2.3 0.0 copy-start.1
  2.3 0.9 copy-done.1
  3.3 0.0 copy-start.2
  3.3 0.9 copy-done.2
  4.2 0.0 copy-start.3
  4.2 0.9 copy-done.3
  5.2 0.0 copy-start.4
  5.2 0.9 copy-done.4
  6.1 0.0 copy-start.5
  6.1 0.9 copy-done.5
  7.1 0.0 copy-start.6
  7.1 0.9 copy-done.6
  8.0 0.0 copy-start.7
  8.0 0.9 copy-done.7
  9.0 0.0 copy-start.8
  9.0 0.8 copy-done.8
  9.7 0.0 copy-start.9
  9.7 0.8 copy-done.9
  10.5 0.0 copy-start.10
  10.5 0.8 copy-done.10
  11.2 0.0 copy-start.11
  11.2 0.8 copy-done.11
  12.0 0.0 copy-start.12
  12.0 0.8 copy-done.12
  12.8 0.0 copy-start.13
  12.8 0.8 copy-done.13
  13.5 84.7 %triangle_backward.1 = (bf16[16,64,128]{2,1,0:T(8,128)(2,1)S(1)}, f32[4,128]{1,0:T(4,128)S(1)}, f32[128,128]{1,0:T(8,128)S(1)}, f32[128,128]{1,0:T(8,128)S(1)}, ...) custom-call(bf16[16,64,128]{2,1,0:T(8,128)(2,1)S(1)} %copy-done, ...), custom_call_target="tpu_custom_call" | custom-call | tf_op jit(solution)/shard_map/triangle_backward/pallas_call | solution.py:305
  98.3 0.5 slice_bitcast_fusion
  98.8 0.7 copy.36
  99.5 0.6 copy.37
  100.1 0.6 copy.38
  100.7 0.6 copy.39
  101.4 0.6 copy.40
  102.0 0.6 copy.41
  102.6 0.6 copy.42
Async XLA Ops:
  0.7 0.7 copy-start.17
  0.7 0.7 copy-start.14
  0.7 0.7 copy-start.15
  0.7 0.7 copy-start.16
  1.4 0.9 copy-start
  2.3 0.9 copy-start.1
  3.3 0.9 copy-start.2
  4.2 0.9 copy-start.3
  5.2 0.9 copy-start.4
  6.1 0.9 copy-start.5
  7.1 0.9 copy-start.6
  8.0 0.9 copy-start.7
  9.0 0.8 copy-start.8
  9.7 0.8 copy-start.9
  10.5 0.8 copy-start.10
  11.2 0.8 copy-start.11
  12.0 0.8 copy-start.12
  12.8 0.8 copy-start.13

commit v2 on v1

v2 whole, which is shorter than its diff:
```python
import jax
import jax.numpy as jnp
from jax import lax
from jax.experimental import pallas as pl
from jax.experimental.pallas import tpu as pltpu
from jax.sharding import PartitionSpec as P

MESH = pl.DeviceIdType.MESH
F32 = jnp.float32
BF16 = jnp.bfloat16
ROWS = 16
COLS = 4
GROUP = ROWS * COLS
TI = 16
TJ = 64
CELLS = TI * TJ
CH = 128
STEP = 2
TURNS = TI // STEP
SPAN = STEP * TJ
SUMMERS = GROUP // 2
BIG = 8


def dot(a, b):
    return jnp.dot(a, b, preferred_element_type=F32)


def dot_nt(a, b):
    return lax.dot_general(a, b, (((1,), (1,)), ((), ())), preferred_element_type=F32)


def dot_tn(a, b):
    return lax.dot_general(a, b, (((0,), (0,)), ((), ())), preferred_element_type=F32)


def sigmoid(x):
    return 1.0 / (1.0 + jnp.exp(-x))


def normalize(values):
    average = jnp.mean(values, axis=-1, keepdims=True)
    centred = values - average
    inverse = lax.rsqrt(jnp.mean(centred * centred, axis=-1, keepdims=True) + 1e-05)
    return centred * inverse, inverse


def norm_back(grad_hat, normed, inverse):
    grad_mean = jnp.mean(grad_hat, axis=-1, keepdims=True)
    grad_corr = jnp.mean(grad_hat * normed, axis=-1, keepdims=True)
    return inverse * (grad_hat - grad_mean - normed * grad_corr)


def fold_rows(x):
    return jnp.sum(x.reshape(-1, 8, CH), axis=0)


def kernel(*refs):
    hbm_in, refs = refs[:18], refs[18:]
    (pair_o, vec_o, *w_o), refs = refs[:8], refs[8:]
    held, refs = refs[:18], refs[18:]
    (pair_act, proj_a, gate_a, proj_b, gate_b, tri_out, gate_out, cotangent,
     gain_in, bias_in, gain_tri, bias_tri,
     w_proj_a, w_gate_a, w_proj_b, w_gate_b, w_out, w_gate) = held
    (tmp, tmp2, left_t, right_t, grad_t, left_r, right_r, grad_r,
     dl_s, dr_s, dl_r, dr_r, rbd,
     sig_a, sig_b, mixed_s, lift_s, ggate_s, normed_s, inv_s, pn_s, pn_t, gn_s, gpg_s, w_a, w_b,
     part, part_r, final, vec_acc, vec_s, vec_r, vec_c, vec_a,
     in_sem, send, recv) = refs
    d, r, c = lax.axis_index("dp"), lax.axis_index("row"), lax.axis_index("col")
    mine = r * COLS + c

    fetches = [pltpu.make_async_copy(hbm_in[n], held[n], in_sem.at[n]) for n in range(18)]
    for n in (4, 3, 5, 6, 7, 16, 10, 11, 2, 1, 0, 8, 9, 17, 12, 13, 14, 15):
        fetches[n].start()

    def need(*ns):
        for n in ns:
            fetches[n].wait()

    def peer_of(k):
        k = jnp.where(k <= 7, k - 1, k)
        n = 7 - lax.rem(k, 8)
        dz = lax.rem(jnp.where(lax.rem(n, 2) == 1, (n + 1) // 2, 8 - n // 2), 8)
        dy = lax.rem(k // 8, 2)
        pr = lax.rem(r // 2 + dz, 8) * 2 + lax.rem(lax.rem(r, 2) + dy, 2)
        return pr, lax.rem(c + k // 16, COLS)

    barrier = pltpu.get_barrier_semaphore()

    def greet(k, _):
        pr, pc = peer_of(k)
        pl.semaphore_signal(barrier, inc=1, device_id=(d, pr, pc), device_id_type=MESH)
        return 0

    lax.fori_loop(1, GROUP, greet, 0)

    lane = lax.broadcasted_iota(jnp.int32, (TJ, CH), 1)
    low = lane < TJ
    row = lax.broadcasted_iota(jnp.int32, (TJ, CH), 0)
    fold = jnp.where(lax.rem(lane, TJ) == row, 1.0, 0.0).astype(BF16)

    def halves(x):
        zero = jnp.zeros_like(x)
        return jnp.concatenate([jnp.where(low, x, zero), jnp.where(low, zero, x)], axis=0)

    def turned(blocks):
        return dot_nt(fold, jnp.concatenate([halves(b) for b in blocks], axis=0).astype(BF16))

    def spread(scratch, s, flat):
        out = turned([flat[h * TJ : (h + 1) * TJ] for h in range(STEP)])
        for h in range(STEP):
            scratch[pl.ds(s * STEP + h, GROUP, stride=TI), :] = out[:, h * CH : (h + 1) * CH]

    def to_peers(count, copy):
        def go(k, _):
            pr, pc = peer_of(k)
            copy(pr, pc)
            return 0

        lax.fori_loop(1, count, go, 0)

    def remote(src, dst, n, pr, pc):
        pltpu.make_async_remote_copy(
            src_ref=src, dst_ref=dst, send_sem=send.at[n], recv_sem=recv.at[n],
            device_id=(d, pr, pc), device_id_type=MESH,
        ).start()

    def scatter(source, target, n):
        to_peers(GROUP, lambda pr, pc: remote(source.at[pr * COLS + pc], target.at[c, r], n, pr, pc))
        target[c, r] = source[mine]

    def scatter_back(source, target, n):
        to_peers(GROUP, lambda pr, pc: remote(source.at[pc, pr], target.at[mine], n, pr, pc))
        target[mine] = source[c, r]

    def wait_for(sem, like, count):
        view = like.at[pl.ds(0, count)]
        pltpu.make_async_copy(view, view, sem).wait()

    def acts(gate, proj, sig, scratch):
        def go(s, _):
            at = pl.ds(s * STEP, STEP)
            sg = sigmoid(gate[at].reshape(SPAN, CH).astype(F32))
            sig[pl.ds(s * SPAN, SPAN), :] = sg
            act = sg * proj[at].reshape(SPAN, CH).astype(F32)
            spread(scratch, s, act.astype(BF16).astype(F32))
            return 0

        lax.fori_loop(0, TURNS, go, 0)

    need(4, 3)
    acts(gate_b, proj_b, sig_b, tmp)
    right_t[...] = tmp[...].astype(BF16).reshape(GROUP, TI, CH)

    need(5, 6, 7, 16, 10, 11)
    g_tri, b_tri = gain_tri[...], bias_tri[...]
    vec_acc[...] = jnp.zeros_like(vec_acc)

    def outer(s, _):
        at, cells = pl.ds(s * STEP, STEP), pl.ds(s * SPAN, SPAN)
        hat, inv = normalize(tri_out[at].reshape(SPAN, CH).astype(F32))
        mixed = (hat * g_tri + b_tri).astype(BF16)
        lifted = dot(mixed, w_out[...])
        sg = sigmoid(gate_out[at].reshape(SPAN, CH).astype(F32))
        up = cotangent[at].reshape(SPAN, CH).astype(F32)
        ups = up * sg
        lift = ups.astype(BF16)
        ggate_s[cells, :] = (ups * lifted * (1.0 - sg)).astype(BF16)
        mixed_s[cells, :] = mixed
        lift_s[cells, :] = lift
        gm = dot_nt(lift, w_out[...])
        vec_acc[0] += fold_rows(gm * hat)
        vec_acc[1] += fold_rows(gm)
        gt = norm_back(gm * g_tri, hat, inv)
        spread(tmp2, s, gt.astype(BF16).astype(F32))
        return 0

    lax.fori_loop(0, TURNS, outer, 0)
    grad_t[...] = tmp2[...].astype(BF16).reshape(GROUP, TI, CH)

    pl.semaphore_wait(barrier, GROUP - 1)
    scatter(right_t, right_r, 0)
    scatter(grad_t, grad_r, 1)

    need(2, 1)
    acts(gate_a, proj_a, sig_a, tmp)
    left_t[...] = tmp[...].astype(BF16).reshape(GROUP, TI, CH)
    scatter(left_t, left_r, 2)

    chunk = r * 2 + c // 2

    def is_summer(odd):
        return lax.rem(r + c + d, 2) == odd

    def to_summers(g, odd):
        def go(k, _):
            n = 7 - lax.rem(k, 8)
            dz = lax.rem(jnp.where(lax.rem(n, 2) == 1, (n + 1) // 2, 8 - n // 2), 8)
            pr = lax.rem(r // 2 + dz, 8) * 2 + lax.rem(lax.rem(r, 2) + lax.rem(k // 8, 2), 2)
            pc = 2 * lax.rem(c // 2 + k // 16, 2) + lax.rem(pr + d + odd, 2)
            there = pr * 2 + pc // 2

            @pl.when(pr * COLS + pc != mine)
            def _():
                remote(part.at[g, there], part_r.at[g, mine], 5 + g, pr, pc)

            return 0

        lax.fori_loop(0, SUMMERS, go, 0)

        @pl.when(is_summer(odd))
        def _():
            part_r[g, mine] = part[g, chunk]

    def sum_up(g, odd):
        @pl.when(is_summer(odd))
        def _():
            wait_for(recv.at[5 + g], part_r.at[g], GROUP - 1)
            final[g, chunk] = jnp.sum(part_r[g], axis=0)
            to_peers(GROUP, lambda pr, pc: remote(final.at[g, chunk], final.at[g, chunk], 8 + g, pr, pc))

    def summed(g, odd):
        @pl.when(is_summer(odd))
        def _():
            wait_for(recv.at[8 + g], final.at[g], SUMMERS - 1)

        @pl.when(jnp.logical_not(is_summer(odd)))
        def _():
            wait_for(recv.at[8 + g], final.at[g], SUMMERS)

    def sums_left(g, odd):
        @pl.when(is_summer(odd))
        def _():
            wait_for(send.at[5 + g], part.at[g], SUMMERS - 1)
            wait_for(send.at[8 + g], part_r.at[g], GROUP - 1)

        @pl.when(jnp.logical_not(is_summer(odd)))
        def _():
            wait_for(send.at[5 + g], part.at[g], SUMMERS)

    odds = (0, 1, 0)
    need(0, 8, 9, 17)
    g_in, b_in = gain_in[...], bias_in[...]

    def first(s, _):
        at, cells = pl.ds(s * STEP, STEP), pl.ds(s * SPAN, SPAN)
        normed, inv = normalize(pair_act[at].reshape(SPAN, CH).astype(F32))
        normed_s[cells, :] = normed
        inv_s[cells, :] = jnp.broadcast_to(inv, (SPAN, CH))
        pn = (normed * g_in + b_in).astype(BF16)
        pn_s[cells, :] = pn
        gn_s[cells, :] = dot_nt(ggate_s[cells, :], w_gate[...])
        return 0

    lax.fori_loop(0, TURNS, first, 0)
    pn_t[...] = pn_s[...].astype(F32).T.astype(BF16)
    part[0, 0:16] = dot_tn(mixed_s[...], lift_s[...]).reshape(16, 8, CH)
    part[0, 16:32] = dot(pn_t[...], ggate_s[...]).reshape(16, 8, CH)
    to_summers(0, odds[0])

    wait_for(recv.at[0], right_t, GROUP - 1)
    for k in range(COLS):
        for j in range(COLS):
            tile = right_r[k, 4 * j : 4 * j + 4].reshape(TJ, CH)
            rbd[j * CH : (j + 1) * CH, k * CH : (k + 1) * CH] = halves(tile.astype(F32)).astype(BF16)
    wait_for(recv.at[1], grad_t, GROUP - 1)
    grads = jnp.concatenate([grad_r[k].reshape(ROWS * TI, CH) for k in range(COLS)], axis=1)
    d_left = dot(grads, rbd[...]).astype(BF16)
    for k in range(COLS):
        dl_s[k] = d_left[:, k * CH : (k + 1) * CH].reshape(ROWS, TI, CH)
    scatter_back(dl_s, dl_r, 3)
    wait_for(recv.at[2], left_t, GROUP - 1)
    lefts = jnp.concatenate([left_r[k].reshape(ROWS * TI, CH) for k in range(COLS)], axis=1)
    d_right = dot_tn(grads, lefts)
    for k in range(COLS):
        for j in range(COLS):
            tile = d_right[j * CH : (j + 1) * CH, k * CH : (k + 1) * CH]
            dr_s[k, 4 * j : 4 * j + 4] = (
                jnp.where(low, tile[:TJ], tile[TJ:]).astype(BF16).reshape(4, TI, CH)
            )
    scatter_back(dr_s, dr_r, 4)
    sum_up(0, odds[0])

    need(12, 13, 14, 15)
    w_a[:, :CH] = w_proj_a[...]
    w_a[:, CH:] = w_gate_a[...]
    w_b[:, :CH] = w_proj_b[...]
    w_b[:, CH:] = w_gate_b[...]

    def side(arr, n, sig, proj, g):
        wait_for(recv.at[n], right_t, GROUP - 1)
        tmp[...] = arr[...].reshape(CELLS, CH).astype(F32)

        def go(s, _):
            at, cells = pl.ds(s * STEP, STEP), pl.ds(s * SPAN, SPAN)
            out = turned([tmp[pl.ds(s * STEP + h, GROUP, stride=TI), :] for h in range(STEP)])
            dd = jnp.concatenate([out[:, h * CH : (h + 1) * CH] for h in range(STEP)], axis=0)
            sg = sig[cells, :]
            ds = dd * sg
            gpg_s[cells, :CH] = ds.astype(BF16)
            gpg_s[cells, CH:] = (ds * proj[at].reshape(SPAN, CH).astype(F32) * (1.0 - sg)).astype(BF16)
            return 0

        lax.fori_loop(0, TURNS, go, 0)
        both = dot(pn_t[...], gpg_s[...])
        part[g, 0:16] = both[:, :CH].reshape(16, 8, CH)
        part[g, 16:32] = both[:, CH:].reshape(16, 8, CH)
        to_summers(g, odds[g])

    side(dl_r, 3, sig_a, proj_a, 1)

    def more(s, _):
        cells = pl.ds(s * SPAN, SPAN)
        gn_s[cells, :] += dot_nt(gpg_s[cells, :], w_a[...])
        return 0

    lax.fori_loop(0, TURNS, more, 0)
    side(dr_r, 4, sig_b, proj_b, 2)

    def last(s, _):
        at, cells = pl.ds(s * STEP, STEP), pl.ds(s * SPAN, SPAN)
        gn = gn_s[cells, :] + dot_nt(gpg_s[cells, :], w_b[...])
        normed = normed_s[cells, :]
        vec_acc[2] += fold_rows(gn * normed)
        vec_acc[3] += fold_rows(gn)
        back = norm_back(gn * g_in, normed, inv_s[cells, :])
        pair_o[at] = back.astype(BF16).reshape(STEP, TJ, CH)
        return 0

    lax.fori_loop(0, TURNS, last, 0)
    for n in range(4):
        vec_s[n : n + 1, :] = jnp.sum(vec_acc[n], axis=0, keepdims=True)
    for k in range(1, COLS):
        remote(vec_s, vec_r.at[c], 11, r, lax.rem(c + k, COLS))
    vec_r[c] = vec_s[...]
    sum_up(1, odds[1])
    wait_for(recv.at[11], vec_r, COLS - 1)
    vec_c[...] = jnp.sum(vec_r[...], axis=0)

    def over_rows(k, _):
        remote(vec_c, vec_a.at[r], 12, lax.rem(r + k, ROWS), c)
        return 0

    lax.fori_loop(1, ROWS, over_rows, 0)
    vec_a[r] = vec_c[...]
    sum_up(2, odds[2])

    wait_for(recv.at[12], vec_a, ROWS - 1)
    vec_o[...] = jnp.sum(vec_a[...], axis=0)
    for g, outs in ((1, (0, 1)), (0, (4, 5)), (2, (2, 3))):
        summed(g, odds[g])
        w_o[outs[0]][...] = final[g, 0:16]
        w_o[outs[1]][...] = final[g, 16:32]
    for n in range(5):
        wait_for(send.at[n], right_t, GROUP - 1)
    for g in range(3):
        sums_left(g, odds[g])
    wait_for(send.at[11], vec_r, COLS - 1)
    wait_for(send.at[12], vec_a, ROWS - 1)


def hand_out(*refs):
    (pair_in, vec_in, *w_in), (pair_o, *vec_o), w_o, sem = refs[:8], refs[8:13], refs[13:19], refs[19]
    copies = [pltpu.make_async_copy(pair_in, pair_o, sem.at[0])]
    for n in range(4):
        copies.append(pltpu.make_async_copy(vec_in.at[pl.ds(n, 1)], vec_o[n], sem.at[1 + n]))
    for n in range(6):
        copies.append(pltpu.make_async_copy(w_in[n], w_o[n], sem.at[5 + n]))
    for copy in copies:
        copy.start()
    for copy in copies:
        copy.wait()


def local(
    pair_act, gain_in, bias_in, proj_a, gate_a, proj_b, gate_b, tri_out, gain_tri, bias_tri,
    gate_out, cotangent, w_proj_a, w_gate_a, w_proj_b, w_gate_b, w_out, w_gate,
):
    args = (
        pair_act, proj_a, gate_a, proj_b, gate_b, tri_out, gate_out, cotangent,
        gain_in.reshape(1, CH), bias_in.reshape(1, CH), gain_tri.reshape(1, CH), bias_tri.reshape(1, CH),
        w_proj_a, w_gate_a, w_proj_b, w_gate_b, w_out, w_gate,
    )
    hbm = pl.BlockSpec(memory_space=pltpu.HBM)
    vmem = pl.BlockSpec(memory_space=pltpu.VMEM)
    square = jax.ShapeDtypeStruct((16, 8, CH), F32)
    turned = pltpu.VMEM((GROUP, TI, CH), BF16)
    landed = pltpu.VMEM((COLS, ROWS, TI, CH), BF16)
    wide = pltpu.VMEM((CELLS, CH), F32)
    half = pltpu.VMEM((CELLS, CH), BF16)
    outs = pl.pallas_call(
        kernel,
        out_shape=(
            jax.ShapeDtypeStruct(pair_act.shape, BF16),
            jax.ShapeDtypeStruct((4, CH), F32),
            square, square, square, square, square, square,
        ),
        in_specs=[hbm] * 18,
        out_specs=tuple([vmem] * 8),
        scratch_shapes=[pltpu.VMEM(a.shape, a.dtype) for a in args] + [
            wide, wide, turned, turned, turned, landed, landed, landed,
            landed, landed, turned, turned, pltpu.VMEM((4 * CH, 4 * CH), BF16),
            wide, wide, half, half, half, wide, wide, half, pltpu.VMEM((CH, CELLS), BF16), wide,
            pltpu.VMEM((CELLS, 2 * CH), BF16), pltpu.VMEM((CH, 2 * CH), BF16), pltpu.VMEM((CH, 2 * CH), BF16),
            pltpu.VMEM((3, SUMMERS, 8, CH), F32), pltpu.VMEM((3, GROUP, 8, CH), F32),
            pltpu.VMEM((3, SUMMERS, 8, CH), F32), pltpu.VMEM((4, 8, CH), F32),
            pltpu.VMEM((4, CH), F32), pltpu.VMEM((COLS, 4, CH), F32),
            pltpu.VMEM((4, CH), F32), pltpu.VMEM((ROWS, 4, CH), F32),
            pltpu.SemaphoreType.DMA((18,)),
            pltpu.SemaphoreType.DMA((13,)), pltpu.SemaphoreType.DMA((13,)),
        ],
        compiler_params=pltpu.CompilerParams(
            collective_id=0, has_side_effects=True, vmem_limit_bytes=63 * 1024 * 1024
        ),
        name="triangle_backward",
    )(*args)
    vector = jax.ShapeDtypeStruct((1, CH), F32)
    pair_grad, v0, v1, v2, v3, *weights = pl.pallas_call(
        hand_out,
        out_shape=(jax.ShapeDtypeStruct(pair_act.shape, BF16),) + (vector,) * 4 + (square,) * 6,
        in_specs=[vmem] * 8,
        out_specs=tuple([hbm] * 11),
        scratch_shapes=[pltpu.SemaphoreType.DMA((11,))],
        name="hand_out",
    )(*outs)
    vecs = [v.reshape(CH) for v in (v2, v3, v0, v1)]
    return (pair_grad, *vecs, *[w.reshape(CH, CH) for w in weights])


def solution(mesh):
    tile = P(("dp", "row"), "col", None)
    placed = (
        tile, P(), P(), tile, tile, tile, tile, tile, P(), P(),
        tile, tile, P(), P(), P(), P(), P(), P(),
    )
    vector, matrix = P("dp"), P("dp", None)
    return jax.shard_map(
        local,
        mesh=mesh,
        in_specs=placed,
        out_specs=(tile,) + (vector,) * 4 + (matrix,) * 6,
        check_vma=False,
    )
```

time: 104 us -> 72.8 us (0.70)
  the two profiles are of different devices: /device:TPU:64 before, /device:TPU:8 now
where the time goes in v2:
time: 72.8 us; the launch traced here: 71.6 us
  Pallas kernels  70.9 us (97%)
    pallas_call x1, Pallas kernels, local(): pl.pallas_call(kernel, out_shape=(jax.ShapeDtypeStruct(pair_act.shape, BF...  68.9 us
    pallas_call x1, Pallas kernels, local(): pl.pallas_call(hand_out, out_shape=(jax.ShapeDtypeStruct(pair_act.shape,...  2.02 us

profile of v2, /device:TPU:8, one launch (start us, length us, event | category | flops | bytes accessed | tf_op | source)
XLA Modules:
  0.0 71.6 jit_solution(15211720835384023520)
XLA Ops:
  0.7 68.9 %triangle_backward.1 = (bf16[16,64,128]{2,1,0:T(8,128)(2,1)}, f32[4,128]{1,0:T(4,128)}, f32[16,8,128]{2,1,0:T(8,128)}, f32[16,8,128]{2,1,0:T(8,128)}, f32[16,8,1...) custom-call(bf16[16,64,128]{2,1,0:T(8,128)(2,1)} %refs_0_.1, ...), custom_call_target="tpu_custom_call" | custom-call | tf_op jit(solution)/shard_map/triangle_backward/pallas_call | solution.py:392
  69.5 2.0 %hand_out.1 = (bf16[16,64,128]{2,1,0:T(8,128)(2,1)}, f32[1,128]{1,0:T(1,128)}, f32[1,128]{1,0:T(1,128)}, f32[1,128]{1,0:T(1,128)}, f32[1,128]{1,0:T(1,128)}, /*i...) custom-call(bf16[16,64,128]{2,1,0:T(8,128)(2,1)} %get-tuple-element., ...), custom_call_target="tpu_custom_call" | custom-call | tf_op jit(solution)/shard_map/hand_out/pallas_call | solution.py:419

commit v3 on v2

--- a/solution.py
+++ b/solution.py
@@ -18,7 +18,6 @@
 STEP = 2
 TURNS = TI // STEP
 SPAN = STEP * TJ
-SUMMERS = GROUP // 2
 BIG = 8
 
 
@@ -79,8 +78,8 @@
             fetches[n].wait()
 
     def peer_of(k):
-        k = jnp.where(k <= 7, k - 1, k)
-        n = 7 - lax.rem(k, 8)
+        k = GROUP - k
+        n = lax.rem(k, 8)
         dz = lax.rem(jnp.where(lax.rem(n, 2) == 1, (n + 1) // 2, 8 - n // 2), 8)
         dy = lax.rem(k // 8, 2)
         pr = lax.rem(r // 2 + dz, 8) * 2 + lax.rem(lax.rem(r, 2) + dy, 2)
@@ -147,11 +146,14 @@
             spread(scratch, s, act.astype(BF16).astype(F32))
             return 0
 
-        lax.fori_loop(0, TURNS, go, 0)
+        lax.fori_loop(0, TURNS, go, 0, unroll=TURNS)
 
     need(4, 3)
     acts(gate_b, proj_b, sig_b, tmp)
     right_t[...] = tmp[...].astype(BF16).reshape(GROUP, TI, CH)
+
+    pl.semaphore_wait(barrier, GROUP - 1)
+    scatter(right_t, right_r, 0)
 
     need(5, 6, 7, 16, 10, 11)
     g_tri, b_tri = gain_tri[...], bias_tri[...]
@@ -176,11 +178,9 @@
         spread(tmp2, s, gt.astype(BF16).astype(F32))
         return 0
 
-    lax.fori_loop(0, TURNS, outer, 0)
+    lax.fori_loop(0, TURNS, outer, 0, unroll=TURNS)
     grad_t[...] = tmp2[...].astype(BF16).reshape(GROUP, TI, CH)
 
-    pl.semaphore_wait(barrier, GROUP - 1)
-    scatter(right_t, right_r, 0)
     scatter(grad_t, grad_r, 1)
 
     need(2, 1)
@@ -188,58 +188,57 @@
     left_t[...] = tmp[...].astype(BF16).reshape(GROUP, TI, CH)
     scatter(left_t, left_r, 2)
 
-    chunk = r * 2 + c // 2
-
-    def is_summer(odd):
-        return lax.rem(r + c + d, 2) == odd
-
-    def to_summers(g, odd):
+    def summer_col(g, on_row):
+        return lax.rem(on_row + on_row // 4 + g + d, COLS)
+
+    def is_summer(g):
+        return c == summer_col(g, r)
+
+    def to_summers(g):
         def go(k, _):
             n = 7 - lax.rem(k, 8)
             dz = lax.rem(jnp.where(lax.rem(n, 2) == 1, (n + 1) // 2, 8 - n // 2), 8)
-            pr = lax.rem(r // 2 + dz, 8) * 2 + lax.rem(lax.rem(r, 2) + lax.rem(k // 8, 2), 2)
-            pc = 2 * lax.rem(c // 2 + k // 16, 2) + lax.rem(pr + d + odd, 2)
-            there = pr * 2 + pc // 2
+            pr = lax.rem(r // 2 + dz, 8) * 2 + lax.rem(lax.rem(r, 2) + k // 8, 2)
+            pc = summer_col(g, pr)
 
             @pl.when(pr * COLS + pc != mine)
             def _():
-                remote(part.at[g, there], part_r.at[g, mine], 5 + g, pr, pc)
+                remote(part.at[g, pr], part_r.at[g, mine], 5 + g, pr, pc)
 
             return 0
 
-        lax.fori_loop(0, SUMMERS, go, 0)
-
-        @pl.when(is_summer(odd))
-        def _():
-            part_r[g, mine] = part[g, chunk]
-
-    def sum_up(g, odd):
-        @pl.when(is_summer(odd))
+        lax.fori_loop(0, ROWS, go, 0)
+
+        @pl.when(is_summer(g))
+        def _():
+            part_r[g, mine] = part[g, r]
+
+    def sum_up(g):
+        @pl.when(is_summer(g))
         def _():
             wait_for(recv.at[5 + g], part_r.at[g], GROUP - 1)
-            final[g, chunk] = jnp.sum(part_r[g], axis=0)
-            to_peers(GROUP, lambda pr, pc: remote(final.at[g, chunk], final.at[g, chunk], 8 + g, pr, pc))
-
-    def summed(g, odd):
-        @pl.when(is_summer(odd))
-        def _():
-            wait_for(recv.at[8 + g], final.at[g], SUMMERS - 1)
-
-        @pl.when(jnp.logical_not(is_summer(odd)))
-        def _():
-            wait_for(recv.at[8 + g], final.at[g], SUMMERS)
-
-    def sums_left(g, odd):
-        @pl.when(is_summer(odd))
-        def _():
-            wait_for(send.at[5 + g], part.at[g], SUMMERS - 1)
+            final[g, r] = jnp.sum(part_r[g].astype(F32), axis=0).astype(final.dtype)
+            to_peers(GROUP, lambda pr, pc: remote(final.at[g, r], final.at[g, r], 8 + g, pr, pc))
+
+    def summed(g):
+        @pl.when(is_summer(g))
+        def _():
+            wait_for(recv.at[8 + g], final.at[g], ROWS - 1)
+
+        @pl.when(jnp.logical_not(is_summer(g)))
+        def _():
+            wait_for(recv.at[8 + g], final.at[g], ROWS)
+
+    def sums_left(g):
+        @pl.when(is_summer(g))
+        def _():
+            wait_for(send.at[5 + g], part.at[g], ROWS - 1)
             wait_for(send.at[8 + g], part_r.at[g], GROUP - 1)
 
-        @pl.when(jnp.logical_not(is_summer(odd)))
-        def _():
-            wait_for(send.at[5 + g], part.at[g], SUMMERS)
-
-    odds = (0, 1, 0)
+        @pl.when(jnp.logical_not(is_summer(g)))
+        def _():
+            wait_for(send.at[5 + g], part.at[g], ROWS)
+
     need(0, 8, 9, 17)
     g_in, b_in = gain_in[...], bias_in[...]
 
@@ -253,11 +252,11 @@
         gn_s[cells, :] = dot_nt(ggate_s[cells, :], w_gate[...])
         return 0
 
-    lax.fori_loop(0, TURNS, first, 0)
+    lax.fori_loop(0, TURNS, first, 0, unroll=TURNS)
     pn_t[...] = pn_s[...].astype(F32).T.astype(BF16)
-    part[0, 0:16] = dot_tn(mixed_s[...], lift_s[...]).reshape(16, 8, CH)
-    part[0, 16:32] = dot(pn_t[...], ggate_s[...]).reshape(16, 8, CH)
-    to_summers(0, odds[0])
+    part[0, 0:8] = dot_tn(mixed_s[...], lift_s[...]).astype(BF16).reshape(8, 16, CH)
+    part[0, 8:16] = dot(pn_t[...], ggate_s[...]).astype(BF16).reshape(8, 16, CH)
+    to_summers(0)
 
     wait_for(recv.at[0], right_t, GROUP - 1)
     for k in range(COLS):
@@ -280,7 +279,7 @@
                 jnp.where(low, tile[:TJ], tile[TJ:]).astype(BF16).reshape(4, TI, CH)
             )
     scatter_back(dr_s, dr_r, 4)
-    sum_up(0, odds[0])
+    sum_up(0)
 
     need(12, 13, 14, 15)
     w_a[:, :CH] = w_proj_a[...]
@@ -302,11 +301,11 @@
             gpg_s[cells, CH:] = (ds * proj[at].reshape(SPAN, CH).astype(F32) * (1.0 - sg)).astype(BF16)
             return 0
 
-        lax.fori_loop(0, TURNS, go, 0)
+        lax.fori_loop(0, TURNS, go, 0, unroll=TURNS)
         both = dot(pn_t[...], gpg_s[...])
-        part[g, 0:16] = both[:, :CH].reshape(16, 8, CH)
-        part[g, 16:32] = both[:, CH:].reshape(16, 8, CH)
-        to_summers(g, odds[g])
+        part[g, 0:8] = both[:, :CH].astype(BF16).reshape(8, 16, CH)
+        part[g, 8:16] = both[:, CH:].astype(BF16).reshape(8, 16, CH)
+        to_summers(g)
 
     side(dl_r, 3, sig_a, proj_a, 1)
 
@@ -315,7 +314,7 @@
         gn_s[cells, :] += dot_nt(gpg_s[cells, :], w_a[...])
         return 0
 
-    lax.fori_loop(0, TURNS, more, 0)
+    lax.fori_loop(0, TURNS, more, 0, unroll=TURNS)
     side(dr_r, 4, sig_b, proj_b, 2)
 
     def last(s, _):
@@ -328,13 +327,13 @@
         pair_o[at] = back.astype(BF16).reshape(STEP, TJ, CH)
         return 0
 
-    lax.fori_loop(0, TURNS, last, 0)
+    lax.fori_loop(0, TURNS, last, 0, unroll=TURNS)
     for n in range(4):
         vec_s[n : n + 1, :] = jnp.sum(vec_acc[n], axis=0, keepdims=True)
     for k in range(1, COLS):
         remote(vec_s, vec_r.at[c], 11, r, lax.rem(c + k, COLS))
     vec_r[c] = vec_s[...]
-    sum_up(1, odds[1])
+    sum_up(1)
     wait_for(recv.at[11], vec_r, COLS - 1)
     vec_c[...] = jnp.sum(vec_r[...], axis=0)
 
@@ -344,18 +343,18 @@
 
     lax.fori_loop(1, ROWS, over_rows, 0)
     vec_a[r] = vec_c[...]
-    sum_up(2, odds[2])
+    sum_up(2)
 
     wait_for(recv.at[12], vec_a, ROWS - 1)
     vec_o[...] = jnp.sum(vec_a[...], axis=0)
     for g, outs in ((1, (0, 1)), (0, (4, 5)), (2, (2, 3))):
-        summed(g, odds[g])
-        w_o[outs[0]][...] = final[g, 0:16]
-        w_o[outs[1]][...] = final[g, 16:32]
+        summed(g)
+        w_o[outs[0]][...] = final[g, 0:8].astype(F32).reshape(CH, CH)
+        w_o[outs[1]][...] = final[g, 8:16].astype(F32).reshape(CH, CH)
     for n in range(5):
         wait_for(send.at[n], right_t, GROUP - 1)
     for g in range(3):
-        sums_left(g, odds[g])
+        sums_left(g)
     wait_for(send.at[11], vec_r, COLS - 1)
     wait_for(send.at[12], vec_a, ROWS - 1)
 
@@ -384,7 +383,7 @@
     )
     hbm = pl.BlockSpec(memory_space=pltpu.HBM)
     vmem = pl.BlockSpec(memory_space=pltpu.VMEM)
-    square = jax.ShapeDtypeStruct((16, 8, CH), F32)
+    square = jax.ShapeDtypeStruct((CH, CH), F32)
     turned = pltpu.VMEM((GROUP, TI, CH), BF16)
     landed = pltpu.VMEM((COLS, ROWS, TI, CH), BF16)
     wide = pltpu.VMEM((CELLS, CH), F32)
@@ -403,8 +402,8 @@
             landed, landed, turned, turned, pltpu.VMEM((4 * CH, 4 * CH), BF16),
             wide, wide, half, half, half, wide, wide, half, pltpu.VMEM((CH, CELLS), BF16), wide,
             pltpu.VMEM((CELLS, 2 * CH), BF16), pltpu.VMEM((CH, 2 * CH), BF16), pltpu.VMEM((CH, 2 * CH), BF16),
-            pltpu.VMEM((3, SUMMERS, 8, CH), F32), pltpu.VMEM((3, GROUP, 8, CH), F32),
-            pltpu.VMEM((3, SUMMERS, 8, CH), F32), pltpu.VMEM((4, 8, CH), F32),
+            pltpu.VMEM((3, ROWS, 16, CH), BF16), pltpu.VMEM((3, GROUP, 16, CH), BF16),
+            pltpu.VMEM((3, ROWS, 16, CH), BF16), pltpu.VMEM((4, 8, CH), F32),
             pltpu.VMEM((4, CH), F32), pltpu.VMEM((COLS, 4, CH), F32),
             pltpu.VMEM((4, CH), F32), pltpu.VMEM((ROWS, 4, CH), F32),
             pltpu.SemaphoreType.DMA((18,)),
@@ -425,7 +424,7 @@
         name="hand_out",
     )(*outs)
     vecs = [v.reshape(CH) for v in (v2, v3, v0, v1)]
-    return (pair_grad, *vecs, *[w.reshape(CH, CH) for w in weights])
+    return (pair_grad, *vecs, *weights)
 
 
 def solution(mesh):

time: 72.8 us -> 65.4 us (0.90); the launches traced: 71.6 us -> 65.3 us
  Pallas kernels: 70.9 us -> 64.6 us
    pallas_call x1, Pallas kernels: 68.9 us -> 62.6 us  [local(): pl.pallas_call(kernel, out_shape=(jax.ShapeDtypeStruct(pair_act.shape, BF...]
where the time goes in v3:
time: 65.4 us; the launch traced here: 65.3 us
  Pallas kernels  64.6 us (99%)
  between operations  0.66 us (1%)
    pallas_call x1, Pallas kernels, local(): pl.pallas_call(kernel, out_shape=(jax.ShapeDtypeStruct(pair_act.shape, BF...  62.6 us
    pallas_call x1, Pallas kernels, local(): pl.pallas_call(hand_out, out_shape=(jax.ShapeDtypeStruct(pair_act.shape,...  2.02 us

profile of v3, /device:TPU:8, one launch (start us, length us, event | category | flops | bytes accessed | tf_op | source)
XLA Modules:
  0.0 65.3 jit_solution(8381184988319464804)
XLA Ops:
  0.7 62.6 %triangle_backward.1 = (bf16[16,64,128]{2,1,0:T(8,128)(2,1)}, f32[4,128]{1,0:T(4,128)}, f32[128,128]{1,0:T(8,128)}, f32[128,128]{1,0:T(8,128)}, f32[128,128]{1,0...) custom-call(bf16[16,64,128]{2,1,0:T(8,128)(2,1)} %refs_0_.1, bf16[16,64,128]{2,1,0:T(8,128)(2,1)} %refs_1_.1, ...), custom_call_target="tpu_custom_call" | custom-call | tf_op jit(solution)/shard_map/triangle_backward/pallas_call | solution.py:391
  63.3 2.0 %hand_out.1 = (bf16[16,64,128]{2,1,0:T(8,128)(2,1)}, f32[1,128]{1,0:T(1,128)}, f32[1,128]{1,0:T(1,128)}, f32[1,128]{1,0:T(1,128)}, f32[1,128]{1,0:T(1,128)}, /*i...) custom-call(bf16[16,64,128]{2,1,0:T(8,128)(2,1)} %get-tuple-element., ...), custom_call_target="tpu_custom_call" | custom-call | tf_op jit(solution)/shard_map/hand_out/pallas_call | solution.py:418

commit v4 on v3

--- a/solution.py
+++ b/solution.py
@@ -50,6 +50,10 @@
     return inverse * (grad_hat - grad_mean - normed * grad_corr)
 
 
+def alternate(n):
+    return lax.rem(jnp.where(lax.rem(n, 2) == 1, (n + 1) // 2, 8 - n // 2), 8)
+
+
 def fold_rows(x):
     return jnp.sum(x.reshape(-1, 8, CH), axis=0)
 
@@ -64,7 +68,8 @@
     (tmp, tmp2, left_t, right_t, grad_t, left_r, right_r, grad_r,
      dl_s, dr_s, dl_r, dr_r, rbd,
      sig_a, sig_b, mixed_s, lift_s, ggate_s, normed_s, inv_s, pn_s, pn_t, gn_s, gpg_s, w_a, w_b,
-     part, part_r, final, vec_acc, vec_s, vec_r, vec_c, vec_a,
+     part, part_r, final, tail_p, tail_z, tail_s, tail_x, tail_t, tail_f,
+     vec_acc, vec_s, vec_r, vec_c, vec_a,
      in_sem, send, recv) = refs
     d, r, c = lax.axis_index("dp"), lax.axis_index("row"), lax.axis_index("col")
     mine = r * COLS + c
@@ -77,22 +82,26 @@
         for n in ns:
             fetches[n].wait()
 
-    def peer_of(k):
-        k = GROUP - k
-        n = lax.rem(k, 8)
-        dz = lax.rem(jnp.where(lax.rem(n, 2) == 1, (n + 1) // 2, 8 - n // 2), 8)
-        dy = lax.rem(k // 8, 2)
-        pr = lax.rem(r // 2 + dz, 8) * 2 + lax.rem(lax.rem(r, 2) + dy, 2)
-        return pr, lax.rem(c + k // 16, COLS)
+    cols = [lax.rem(c + k, COLS) for k in range(COLS)]
+
+    def to_peers(copy):
+        def go(k, _):
+            k = ROWS - k
+            pr = lax.rem(r // 2 + alternate(lax.rem(k, 8)), 8) * 2 + lax.rem(lax.rem(r, 2) + k // 8, 2)
+            for n in (2, 1, 3, 0):
+                copy(pr, cols[n])
+            return 0
+
+        lax.fori_loop(1, ROWS, go, 0)
+        for n in (2, 1, 3):
+            copy(r, cols[n])
 
     barrier = pltpu.get_barrier_semaphore()
 
-    def greet(k, _):
-        pr, pc = peer_of(k)
+    def greet(pr, pc):
         pl.semaphore_signal(barrier, inc=1, device_id=(d, pr, pc), device_id_type=MESH)
-        return 0
-
-    lax.fori_loop(1, GROUP, greet, 0)
+
+    to_peers(greet)
 
     lane = lax.broadcasted_iota(jnp.int32, (TJ, CH), 1)
     low = lane < TJ
@@ -110,14 +119,6 @@
         out = turned([flat[h * TJ : (h + 1) * TJ] for h in range(STEP)])
         for h in range(STEP):
             scratch[pl.ds(s * STEP + h, GROUP, stride=TI), :] = out[:, h * CH : (h + 1) * CH]
-
-    def to_peers(count, copy):
-        def go(k, _):
-            pr, pc = peer_of(k)
-            copy(pr, pc)
-            return 0
-
-        lax.fori_loop(1, count, go, 0)
 
     def remote(src, dst, n, pr, pc):
         pltpu.make_async_remote_copy(
@@ -126,11 +127,11 @@
         ).start()
 
     def scatter(source, target, n):
-        to_peers(GROUP, lambda pr, pc: remote(source.at[pr * COLS + pc], target.at[c, r], n, pr, pc))
+        to_peers(lambda pr, pc: remote(source.at[pr * COLS + pc], target.at[c, r], n, pr, pc))
         target[c, r] = source[mine]
 
     def scatter_back(source, target, n):
-        to_peers(GROUP, lambda pr, pc: remote(source.at[pc, pr], target.at[mine], n, pr, pc))
+        to_peers(lambda pr, pc: remote(source.at[pc, pr], target.at[mine], n, pr, pc))
         target[mine] = source[c, r]
 
     def wait_for(sem, like, count):
@@ -197,7 +198,7 @@
     def to_summers(g):
         def go(k, _):
             n = 7 - lax.rem(k, 8)
-            dz = lax.rem(jnp.where(lax.rem(n, 2) == 1, (n + 1) // 2, 8 - n // 2), 8)
+            dz = alternate(n)
             pr = lax.rem(r // 2 + dz, 8) * 2 + lax.rem(lax.rem(r, 2) + k // 8, 2)
             pc = summer_col(g, pr)
 
@@ -218,7 +219,7 @@
         def _():
             wait_for(recv.at[5 + g], part_r.at[g], GROUP - 1)
             final[g, r] = jnp.sum(part_r[g].astype(F32), axis=0).astype(final.dtype)
-            to_peers(GROUP, lambda pr, pc: remote(final.at[g, r], final.at[g, r], 8 + g, pr, pc))
+            to_peers(lambda pr, pc: remote(final.at[g, r], final.at[g, r], 8 + g, pr, pc))
 
     def summed(g):
         @pl.when(is_summer(g))
@@ -287,7 +288,7 @@
     w_b[:, :CH] = w_proj_b[...]
     w_b[:, CH:] = w_gate_b[...]
 
-    def side(arr, n, sig, proj, g):
+    def side(arr, n, sig, proj):
         wait_for(recv.at[n], right_t, GROUP - 1)
         tmp[...] = arr[...].reshape(CELLS, CH).astype(F32)
 
@@ -302,12 +303,28 @@
             return 0
 
         lax.fori_loop(0, TURNS, go, 0, unroll=TURNS)
-        both = dot(pn_t[...], gpg_s[...])
-        part[g, 0:8] = both[:, :CH].astype(BF16).reshape(8, 16, CH)
-        part[g, 8:16] = both[:, CH:].astype(BF16).reshape(8, 16, CH)
-        to_summers(g)
-
-    side(dl_r, 3, sig_a, proj_a, 1)
+        return dot(pn_t[...], gpg_s[...]).astype(BF16)
+
+    z, y = r // 2, lax.rem(r, 2)
+    in_plane = y * COLS + c
+
+    def along_z(src_of, dst, n):
+        def go(k, _):
+            pz = lax.rem(z + alternate(8 - k), 8)
+            remote(src_of(pz), dst.at[z], n, pz * 2 + y, c)
+            return 0
+
+        lax.fori_loop(1, 8, go, 0)
+
+    def over_plane(src, dst, n):
+        for k in (6, 5, 7, 4, 2, 1, 3):
+            remote(src, dst.at[in_plane], n, z * 2 + lax.rem(y + k // COLS, 2), lax.rem(c + k % COLS, COLS))
+
+    both = side(dl_r, 3, sig_a, proj_a)
+    tail_p[0, 0:4] = both[:, :CH].reshape(4, 32, CH)
+    tail_p[0, 4:8] = both[:, CH:].reshape(4, 32, CH)
+    along_z(lambda pz: tail_p.at[0, pz], tail_z.at[0], 6)
+    tail_z[0, z] = tail_p[0, z]
 
     def more(s, _):
         cells = pl.ds(s * SPAN, SPAN)
@@ -315,7 +332,11 @@
         return 0
 
     lax.fori_loop(0, TURNS, more, 0, unroll=TURNS)
-    side(dr_r, 4, sig_b, proj_b, 2)
+    both = side(dr_r, 4, sig_b, proj_b)
+    tail_p[1, 0:4] = both[:, :CH].reshape(4, 32, CH)
+    tail_p[1, 4:8] = both[:, CH:].reshape(4, 32, CH)
+    along_z(lambda pz: tail_p.at[1, pz], tail_z.at[1], 7)
+    tail_z[1, z] = tail_p[1, z]
 
     def last(s, _):
         at, cells = pl.ds(s * STEP, STEP), pl.ds(s * SPAN, SPAN)
@@ -333,7 +354,11 @@
     for k in range(1, COLS):
         remote(vec_s, vec_r.at[c], 11, r, lax.rem(c + k, COLS))
     vec_r[c] = vec_s[...]
-    sum_up(1)
+    wait_for(recv.at[6], tail_p.at[0], 7)
+    wait_for(recv.at[7], tail_p.at[1], 7)
+    tail_s[...] = jnp.sum(tail_z[...].astype(F32), axis=1).astype(BF16)
+    over_plane(tail_s, tail_x, 10)
+    tail_x[in_plane] = tail_s[...]
     wait_for(recv.at[11], vec_r, COLS - 1)
     vec_c[...] = jnp.sum(vec_r[...], axis=0)
 
@@ -343,18 +368,26 @@
 
     lax.fori_loop(1, ROWS, over_rows, 0)
     vec_a[r] = vec_c[...]
-    sum_up(2)
-
+    wait_for(recv.at[10], tail_x, 7)
+    tail_t[...] = jnp.sum(tail_x[...].astype(F32), axis=0).astype(BF16)
+    along_z(lambda pz: tail_t, tail_f, 13)
+    tail_f[z] = tail_t[...]
     wait_for(recv.at[12], vec_a, ROWS - 1)
     vec_o[...] = jnp.sum(vec_a[...], axis=0)
-    for g, outs in ((1, (0, 1)), (0, (4, 5)), (2, (2, 3))):
+    for g, outs in ((0, (4, 5)),):
         summed(g)
         w_o[outs[0]][...] = final[g, 0:8].astype(F32).reshape(CH, CH)
         w_o[outs[1]][...] = final[g, 8:16].astype(F32).reshape(CH, CH)
+    wait_for(recv.at[13], tail_x, 7)
+    for n in range(4):
+        w_o[n][...] = tail_f[4 * (n % 2) : 4 * (n % 2) + 4, n // 2].astype(F32).reshape(CH, CH)
+    for n in range(2):
+        wait_for(send.at[6 + n], tail_p.at[n], 7)
+    for n in (10, 13):
+        wait_for(send.at[n], tail_x, 7)
     for n in range(5):
         wait_for(send.at[n], right_t, GROUP - 1)
-    for g in range(3):
-        sums_left(g)
+    sums_left(0)
     wait_for(send.at[11], vec_r, COLS - 1)
     wait_for(send.at[12], vec_a, ROWS - 1)
 
@@ -387,6 +420,7 @@
     turned = pltpu.VMEM((GROUP, TI, CH), BF16)
     landed = pltpu.VMEM((COLS, ROWS, TI, CH), BF16)
     wide = pltpu.VMEM((CELLS, CH), F32)
+    eight = pltpu.VMEM((8, 2, 32, CH), BF16)
     half = pltpu.VMEM((CELLS, CH), BF16)
     outs = pl.pallas_call(
         kernel,
@@ -402,12 +436,15 @@
             landed, landed, turned, turned, pltpu.VMEM((4 * CH, 4 * CH), BF16),
             wide, wide, half, half, half, wide, wide, half, pltpu.VMEM((CH, CELLS), BF16), wide,
             pltpu.VMEM((CELLS, 2 * CH), BF16), pltpu.VMEM((CH, 2 * CH), BF16), pltpu.VMEM((CH, 2 * CH), BF16),
-            pltpu.VMEM((3, ROWS, 16, CH), BF16), pltpu.VMEM((3, GROUP, 16, CH), BF16),
-            pltpu.VMEM((3, ROWS, 16, CH), BF16), pltpu.VMEM((4, 8, CH), F32),
+            pltpu.VMEM((1, ROWS, 16, CH), BF16), pltpu.VMEM((1, GROUP, 16, CH), BF16),
+            pltpu.VMEM((1, ROWS, 16, CH), BF16),
+            pltpu.VMEM((2, 8, 32, CH), BF16), pltpu.VMEM((2, 8, 32, CH), BF16), pltpu.VMEM((2, 32, CH), BF16), eight,
+            pltpu.VMEM((2, 32, CH), BF16), eight,
+            pltpu.VMEM((4, 8, CH), F32),
             pltpu.VMEM((4, CH), F32), pltpu.VMEM((COLS, 4, CH), F32),
             pltpu.VMEM((4, CH), F32), pltpu.VMEM((ROWS, 4, CH), F32),
             pltpu.SemaphoreType.DMA((18,)),
-            pltpu.SemaphoreType.DMA((13,)), pltpu.SemaphoreType.DMA((13,)),
+            pltpu.SemaphoreType.DMA((14,)), pltpu.SemaphoreType.DMA((14,)),
         ],
         compiler_params=pltpu.CompilerParams(
             collective_id=0, has_side_effects=True, vmem_limit_bytes=63 * 1024 * 1024

time: 65.4 us -> 62.9 us (0.962)
  Pallas kernels: 64.6 us -> 62 us
    pallas_call x1, Pallas kernels: 62.6 us -> 60 us  [local(): pl.pallas_call(kernel, out_shape=(jax.ShapeDtypeStruct(pair_act.shape, BF...]
where the time goes in v4:
time: 62.9 us; the launch traced here: 62.6 us
  Pallas kernels  62 us (99%)
  between operations  0.66 us (1%)
    pallas_call x1, Pallas kernels, local(): pl.pallas_call(kernel, out_shape=(jax.ShapeDtypeStruct(pair_act.shape, BF...  60 us
    pallas_call x1, Pallas kernels, local(): pl.pallas_call(hand_out, out_shape=(jax.ShapeDtypeStruct(pair_act.shape,...  2.02 us

profile of v4, /device:TPU:8, one launch (start us, length us, event | category | flops | bytes accessed | tf_op | source)
XLA Modules:
  0.0 62.6 jit_solution(11804844215482411559)
XLA Ops:
  0.7 60.0 %triangle_backward.1 = (bf16[16,64,128]{2,1,0:T(8,128)(2,1)}, f32[4,128]{1,0:T(4,128)}, f32[128,128]{1,0:T(8,128)}, f32[128,128]{1,0:T(8,128)}, f32[128,128]{1,0...) custom-call(bf16[16,64,128]{2,1,0:T(8,128)(2,1)} %refs_0_.1, bf16[16,64,128]{2,1,0:T(8,128)(2,1)} %refs_1_.1, ...), custom_call_target="tpu_custom_call" | custom-call | tf_op jit(solution)/shard_map/triangle_backward/pallas_call | solution.py:425
  60.6 2.0 %hand_out.1 = (bf16[16,64,128]{2,1,0:T(8,128)(2,1)}, f32[1,128]{1,0:T(1,128)}, f32[1,128]{1,0:T(1,128)}, f32[1,128]{1,0:T(1,128)}, f32[1,128]{1,0:T(1,128)}, /*i...) custom-call(bf16[16,64,128]{2,1,0:T(8,128)(2,1)} %get-tuple-element., ...), custom_call_target="tpu_custom_call" | custom-call | tf_op jit(solution)/shard_map/hand_out/pallas_call | solution.py:455

commit v5 on v4

--- a/solution.py
+++ b/solution.py
@@ -68,14 +68,13 @@
     (tmp, tmp2, left_t, right_t, grad_t, left_r, right_r, grad_r,
      dl_s, dr_s, dl_r, dr_r, rbd,
      sig_a, sig_b, mixed_s, lift_s, ggate_s, normed_s, inv_s, pn_s, pn_t, gn_s, gpg_s, w_a, w_b,
-     part, part_r, final, tail_p, tail_z, tail_s, tail_x, tail_t, tail_f,
-     vec_acc, vec_s, vec_r, vec_c, vec_a,
+     sum_p, sum_x, sum_s, sum_z, sum_t, sum_f, vec_acc, vec_s, vec_r, vec_c, vec_a,
      in_sem, send, recv) = refs
     d, r, c = lax.axis_index("dp"), lax.axis_index("row"), lax.axis_index("col")
     mine = r * COLS + c
 
     fetches = [pltpu.make_async_copy(hbm_in[n], held[n], in_sem.at[n]) for n in range(18)]
-    for n in (4, 3, 5, 6, 7, 16, 10, 11, 2, 1, 0, 8, 9, 17, 12, 13, 14, 15):
+    for n in (4, 3):
         fetches[n].start()
 
     def need(*ns):
@@ -102,6 +101,8 @@
         pl.semaphore_signal(barrier, inc=1, device_id=(d, pr, pc), device_id_type=MESH)
 
     to_peers(greet)
+    for n in (5, 6, 7, 16, 10, 11, 2, 1, 0, 8, 9, 17, 12, 13, 14, 15):
+        fetches[n].start()
 
     lane = lax.broadcasted_iota(jnp.int32, (TJ, CH), 1)
     low = lane < TJ
@@ -189,56 +190,44 @@
     left_t[...] = tmp[...].astype(BF16).reshape(GROUP, TI, CH)
     scatter(left_t, left_r, 2)
 
-    def summer_col(g, on_row):
-        return lax.rem(on_row + on_row // 4 + g + d, COLS)
-
-    def is_summer(g):
-        return c == summer_col(g, r)
-
-    def to_summers(g):
+    z, y = r // 2, lax.rem(r, 2)
+    in_plane = y * COLS + c
+
+    def along_z(src_of, dst, n):
         def go(k, _):
-            n = 7 - lax.rem(k, 8)
-            dz = alternate(n)
-            pr = lax.rem(r // 2 + dz, 8) * 2 + lax.rem(lax.rem(r, 2) + k // 8, 2)
-            pc = summer_col(g, pr)
-
-            @pl.when(pr * COLS + pc != mine)
-            def _():
-                remote(part.at[g, pr], part_r.at[g, mine], 5 + g, pr, pc)
-
+            pz = lax.rem(z + alternate(8 - k), 8)
+            remote(src_of(pz), dst.at[z], n, pz * 2 + y, c)
             return 0
 
-        lax.fori_loop(0, ROWS, go, 0)
-
-        @pl.when(is_summer(g))
-        def _():
-            part_r[g, mine] = part[g, r]
-
-    def sum_up(g):
-        @pl.when(is_summer(g))
-        def _():
-            wait_for(recv.at[5 + g], part_r.at[g], GROUP - 1)
-            final[g, r] = jnp.sum(part_r[g].astype(F32), axis=0).astype(final.dtype)
-            to_peers(lambda pr, pc: remote(final.at[g, r], final.at[g, r], 8 + g, pr, pc))
-
-    def summed(g):
-        @pl.when(is_summer(g))
-        def _():
-            wait_for(recv.at[8 + g], final.at[g], ROWS - 1)
-
-        @pl.when(jnp.logical_not(is_summer(g)))
-        def _():
-            wait_for(recv.at[8 + g], final.at[g], ROWS)
-
-    def sums_left(g):
-        @pl.when(is_summer(g))
-        def _():
-            wait_for(send.at[5 + g], part.at[g], ROWS - 1)
-            wait_for(send.at[8 + g], part_r.at[g], GROUP - 1)
-
-        @pl.when(jnp.logical_not(is_summer(g)))
-        def _():
-            wait_for(send.at[5 + g], part.at[g], ROWS)
+        lax.fori_loop(1, 8, go, 0)
+
+    def over_plane(src_of, dst, n):
+        for k in (6, 5, 7, 4, 2, 1, 3):
+            py, pc = lax.rem(y + k // COLS, 2), cols[k % COLS]
+            remote(src_of(py * COLS + pc), dst.at[in_plane], n, z * 2 + py, pc)
+
+    def place(g, top, bottom):
+        sum_p[g, 0:4] = top.astype(BF16).reshape(4, 32, CH)
+        sum_p[g, 4:8] = bottom.astype(BF16).reshape(4, 32, CH)
+        over_plane(lambda p: sum_p.at[g, p], sum_x.at[g], 5 + g)
+        sum_x[g, in_plane] = sum_p[g, in_plane]
+
+    def cross(g):
+        wait_for(recv.at[5 + g], sum_p.at[g], 7)
+        sum_s[g] = jnp.sum(sum_x[g].astype(F32), axis=0).astype(BF16)
+        along_z(lambda pz: sum_s.at[g], sum_z.at[g], 8 + g)
+        sum_z[g, z] = sum_s[g]
+
+    def share(g):
+        wait_for(recv.at[8 + g], sum_p.at[g], 7)
+        sum_t[g] = jnp.sum(sum_z[g].astype(F32), axis=0).astype(BF16)
+        over_plane(lambda p: sum_t.at[g], sum_f.at[g], 13 + g)
+        sum_f[g, in_plane] = sum_t[g]
+
+    def finish(g, top, bottom):
+        wait_for(recv.at[13 + g], sum_p.at[g], 7)
+        top[...] = sum_f[g, 0:4].astype(F32).reshape(CH, CH)
+        bottom[...] = sum_f[g, 4:8].astype(F32).reshape(CH, CH)
 
     need(0, 8, 9, 17)
     g_in, b_in = gain_in[...], bias_in[...]
@@ -255,9 +244,7 @@
 
     lax.fori_loop(0, TURNS, first, 0, unroll=TURNS)
     pn_t[...] = pn_s[...].astype(F32).T.astype(BF16)
-    part[0, 0:8] = dot_tn(mixed_s[...], lift_s[...]).astype(BF16).reshape(8, 16, CH)
-    part[0, 8:16] = dot(pn_t[...], ggate_s[...]).astype(BF16).reshape(8, 16, CH)
-    to_summers(0)
+    place(0, dot_tn(mixed_s[...], lift_s[...]), dot(pn_t[...], ggate_s[...]))
 
     wait_for(recv.at[0], right_t, GROUP - 1)
     for k in range(COLS):
@@ -270,6 +257,7 @@
     for k in range(COLS):
         dl_s[k] = d_left[:, k * CH : (k + 1) * CH].reshape(ROWS, TI, CH)
     scatter_back(dl_s, dl_r, 3)
+    cross(0)
     wait_for(recv.at[2], left_t, GROUP - 1)
     lefts = jnp.concatenate([left_r[k].reshape(ROWS * TI, CH) for k in range(COLS)], axis=1)
     d_right = dot_tn(grads, lefts)
@@ -280,7 +268,7 @@
                 jnp.where(low, tile[:TJ], tile[TJ:]).astype(BF16).reshape(4, TI, CH)
             )
     scatter_back(dr_s, dr_r, 4)
-    sum_up(0)
+    share(0)
 
     need(12, 13, 14, 15)
     w_a[:, :CH] = w_proj_a[...]
@@ -303,28 +291,10 @@
             return 0
 
         lax.fori_loop(0, TURNS, go, 0, unroll=TURNS)
-        return dot(pn_t[...], gpg_s[...]).astype(BF16)
-
-    z, y = r // 2, lax.rem(r, 2)
-    in_plane = y * COLS + c
-
-    def along_z(src_of, dst, n):
-        def go(k, _):
-            pz = lax.rem(z + alternate(8 - k), 8)
-            remote(src_of(pz), dst.at[z], n, pz * 2 + y, c)
-            return 0
-
-        lax.fori_loop(1, 8, go, 0)
-
-    def over_plane(src, dst, n):
-        for k in (6, 5, 7, 4, 2, 1, 3):
-            remote(src, dst.at[in_plane], n, z * 2 + lax.rem(y + k // COLS, 2), lax.rem(c + k % COLS, COLS))
+        return dot(pn_t[...], gpg_s[...])
 
     both = side(dl_r, 3, sig_a, proj_a)
-    tail_p[0, 0:4] = both[:, :CH].reshape(4, 32, CH)
-    tail_p[0, 4:8] = both[:, CH:].reshape(4, 32, CH)
-    along_z(lambda pz: tail_p.at[0, pz], tail_z.at[0], 6)
-    tail_z[0, z] = tail_p[0, z]
+    place(1, both[:, :CH], both[:, CH:])
 
     def more(s, _):
         cells = pl.ds(s * SPAN, SPAN)
@@ -333,10 +303,7 @@
 
     lax.fori_loop(0, TURNS, more, 0, unroll=TURNS)
     both = side(dr_r, 4, sig_b, proj_b)
-    tail_p[1, 0:4] = both[:, :CH].reshape(4, 32, CH)
-    tail_p[1, 4:8] = both[:, CH:].reshape(4, 32, CH)
-    along_z(lambda pz: tail_p.at[1, pz], tail_z.at[1], 7)
-    tail_z[1, z] = tail_p[1, z]
+    place(2, both[:, :CH], both[:, CH:])
 
     def last(s, _):
         at, cells = pl.ds(s * STEP, STEP), pl.ds(s * SPAN, SPAN)
@@ -354,11 +321,8 @@
     for k in range(1, COLS):
         remote(vec_s, vec_r.at[c], 11, r, lax.rem(c + k, COLS))
     vec_r[c] = vec_s[...]
-    wait_for(recv.at[6], tail_p.at[0], 7)
-    wait_for(recv.at[7], tail_p.at[1], 7)
-    tail_s[...] = jnp.sum(tail_z[...].astype(F32), axis=1).astype(BF16)
-    over_plane(tail_s, tail_x, 10)
-    tail_x[in_plane] = tail_s[...]
+    cross(1)
+    cross(2)
     wait_for(recv.at[11], vec_r, COLS - 1)
     vec_c[...] = jnp.sum(vec_r[...], axis=0)
 
@@ -368,26 +332,18 @@
 
     lax.fori_loop(1, ROWS, over_rows, 0)
     vec_a[r] = vec_c[...]
-    wait_for(recv.at[10], tail_x, 7)
-    tail_t[...] = jnp.sum(tail_x[...].astype(F32), axis=0).astype(BF16)
-    along_z(lambda pz: tail_t, tail_f, 13)
-    tail_f[z] = tail_t[...]
+    share(1)
+    share(2)
     wait_for(recv.at[12], vec_a, ROWS - 1)
     vec_o[...] = jnp.sum(vec_a[...], axis=0)
-    for g, outs in ((0, (4, 5)),):
-        summed(g)
-        w_o[outs[0]][...] = final[g, 0:8].astype(F32).reshape(CH, CH)
-        w_o[outs[1]][...] = final[g, 8:16].astype(F32).reshape(CH, CH)
-    wait_for(recv.at[13], tail_x, 7)
-    for n in range(4):
-        w_o[n][...] = tail_f[4 * (n % 2) : 4 * (n % 2) + 4, n // 2].astype(F32).reshape(CH, CH)
-    for n in range(2):
-        wait_for(send.at[6 + n], tail_p.at[n], 7)
-    for n in (10, 13):
-        wait_for(send.at[n], tail_x, 7)
+    finish(0, w_o[4], w_o[5])
+    finish(1, w_o[0], w_o[1])
+    finish(2, w_o[2], w_o[3])
+    for g in range(3):
+        for n in (5, 8, 13):
+            wait_for(send.at[n + g], sum_p.at[g], 7)
     for n in range(5):
         wait_for(send.at[n], right_t, GROUP - 1)
-    sums_left(0)
     wait_for(send.at[11], vec_r, COLS - 1)
     wait_for(send.at[12], vec_a, ROWS - 1)
 
@@ -420,7 +376,8 @@
     turned = pltpu.VMEM((GROUP, TI, CH), BF16)
     landed = pltpu.VMEM((COLS, ROWS, TI, CH), BF16)
     wide = pltpu.VMEM((CELLS, CH), F32)
-    eight = pltpu.VMEM((8, 2, 32, CH), BF16)
+    eight = pltpu.VMEM((3, 8, 32, CH), BF16)
+    one = pltpu.VMEM((3, 32, CH), BF16)
     half = pltpu.VMEM((CELLS, CH), BF16)
     outs = pl.pallas_call(
         kernel,
@@ -436,15 +393,12 @@
             landed, landed, turned, turned, pltpu.VMEM((4 * CH, 4 * CH), BF16),
             wide, wide, half, half, half, wide, wide, half, pltpu.VMEM((CH, CELLS), BF16), wide,
             pltpu.VMEM((CELLS, 2 * CH), BF16), pltpu.VMEM((CH, 2 * CH), BF16), pltpu.VMEM((CH, 2 * CH), BF16),
-            pltpu.VMEM((1, ROWS, 16, CH), BF16), pltpu.VMEM((1, GROUP, 16, CH), BF16),
-            pltpu.VMEM((1, ROWS, 16, CH), BF16),
-            pltpu.VMEM((2, 8, 32, CH), BF16), pltpu.VMEM((2, 8, 32, CH), BF16), pltpu.VMEM((2, 32, CH), BF16), eight,
-            pltpu.VMEM((2, 32, CH), BF16), eight,
+            eight, eight, one, eight, one, eight,
             pltpu.VMEM((4, 8, CH), F32),
             pltpu.VMEM((4, CH), F32), pltpu.VMEM((COLS, 4, CH), F32),
             pltpu.VMEM((4, CH), F32), pltpu.VMEM((ROWS, 4, CH), F32),
             pltpu.SemaphoreType.DMA((18,)),
-            pltpu.SemaphoreType.DMA((14,)), pltpu.SemaphoreType.DMA((14,)),
+            pltpu.SemaphoreType.DMA((16,)), pltpu.SemaphoreType.DMA((16,)),
         ],
         compiler_params=pltpu.CompilerParams(
             collective_id=0, has_side_effects=True, vmem_limit_bytes=63 * 1024 * 1024

time: 62.9 us -> 62.5 us (level)
  no operation moved by 1% of the time
where the time goes in v5:
time: 62.5 us; the launch traced here: 62.2 us
  Pallas kernels  61.5 us (98%)
  between operations  0.66 us (1%)
    pallas_call x1, Pallas kernels, local(): pl.pallas_call(kernel, out_shape=(jax.ShapeDtypeStruct(pair_act.shape, BF...  59.5 us
    pallas_call x1, Pallas kernels, local(): pl.pallas_call(hand_out, out_shape=(jax.ShapeDtypeStruct(pair_act.shape,...  2.02 us

profile of v5, /device:TPU:8, one launch (start us, length us, event | category | flops | bytes accessed | tf_op | source)
XLA Modules:
  0.0 62.2 jit_solution(7289082015812399834)
XLA Ops:
  0.7 59.5 %triangle_backward.1 = (bf16[16,64,128]{2,1,0:T(8,128)(2,1)}, f32[4,128]{1,0:T(4,128)}, f32[128,128]{1,0:T(8,128)}, f32[128,128]{1,0:T(8,128)}, f32[128,128]{1,0...) custom-call(bf16[16,64,128]{2,1,0:T(8,128)(2,1)} %refs_0_.1, bf16[16,64,128]{2,1,0:T(8,128)(2,1)} %refs_1_.1, ...), custom_call_target="tpu_custom_call" | custom-call | tf_op jit(solution)/shard_map/triangle_backward/pallas_call | solution.py:382
  60.2 2.0 %hand_out.1 = (bf16[16,64,128]{2,1,0:T(8,128)(2,1)}, f32[1,128]{1,0:T(1,128)}, f32[1,128]{1,0:T(1,128)}, f32[1,128]{1,0:T(1,128)}, f32[1,128]{1,0:T(1,128)}, /*i...) custom-call(bf16[16,64,128]{2,1,0:T(8,128)(2,1)} %get-tuple-element., ...), custom_call_target="tpu_custom_call" | custom-call | tf_op jit(solution)/shard_map/hand_out/pallas_call | solution.py:409

commit v6 on v5

--- a/solution.py
+++ b/solution.py
@@ -74,8 +74,13 @@
     mine = r * COLS + c
 
     fetches = [pltpu.make_async_copy(hbm_in[n], held[n], in_sem.at[n]) for n in range(18)]
-    for n in (4, 3):
-        fetches[n].start()
+    first_half = []
+    for q in range(2):
+        piece = pl.ds(q * TI // 2, TI // 2)
+        for n in (4, 3):
+            first_half.append(pltpu.make_async_copy(hbm_in[n].at[piece], held[n].at[piece], in_sem.at[n if q == 0 else n + 15]))
+    for copy in first_half:
+        copy.start()
 
     def need(*ns):
         for n in ns:
@@ -139,7 +144,7 @@
         view = like.at[pl.ds(0, count)]
         pltpu.make_async_copy(view, view, sem).wait()
 
-    def acts(gate, proj, sig, scratch):
+    def acts(gate, proj, sig, scratch, begin=0, end=TURNS):
         def go(s, _):
             at = pl.ds(s * STEP, STEP)
             sg = sigmoid(gate[at].reshape(SPAN, CH).astype(F32))
@@ -148,10 +153,12 @@
             spread(scratch, s, act.astype(BF16).astype(F32))
             return 0
 
-        lax.fori_loop(0, TURNS, go, 0, unroll=TURNS)
-
-    need(4, 3)
-    acts(gate_b, proj_b, sig_b, tmp)
+        lax.fori_loop(begin, end, go, 0, unroll=end - begin)
+
+    for q in range(2):
+        for copy in first_half[2 * q : 2 * q + 2]:
+            copy.wait()
+        acts(gate_b, proj_b, sig_b, tmp, q * TURNS // 2, (q + 1) * TURNS // 2)
     right_t[...] = tmp[...].astype(BF16).reshape(GROUP, TI, CH)
 
     pl.semaphore_wait(barrier, GROUP - 1)
@@ -397,7 +404,7 @@
             pltpu.VMEM((4, 8, CH), F32),
             pltpu.VMEM((4, CH), F32), pltpu.VMEM((COLS, 4, CH), F32),
             pltpu.VMEM((4, CH), F32), pltpu.VMEM((ROWS, 4, CH), F32),
-            pltpu.SemaphoreType.DMA((18,)),
+            pltpu.SemaphoreType.DMA((20,)),
             pltpu.SemaphoreType.DMA((16,)), pltpu.SemaphoreType.DMA((16,)),
         ],
         compiler_params=pltpu.CompilerParams(

time: 62.5 us -> 62.5 us (level)
  no operation moved by 1% of the time
where the time goes in v6:
time: 62.5 us; the launch traced here: 62.2 us
  Pallas kernels  61.5 us (98%)
  between operations  0.66 us (1%)
    pallas_call x1, Pallas kernels, local(): pl.pallas_call(kernel, out_shape=(jax.ShapeDtypeStruct(pair_act.shape, BF...  59.5 us
    pallas_call x1, Pallas kernels, local(): pl.pallas_call(hand_out, out_shape=(jax.ShapeDtypeStruct(pair_act.shape,...  2.02 us

profile of v6, /device:TPU:8, one launch (start us, length us, event | category | flops | bytes accessed | tf_op | source)
XLA Modules:
  0.0 62.2 jit_solution(577628817165790158)
XLA Ops:
  0.7 59.5 %triangle_backward.1 = (bf16[16,64,128]{2,1,0:T(8,128)(2,1)}, f32[4,128]{1,0:T(4,128)}, f32[128,128]{1,0:T(8,128)}, f32[128,128]{1,0:T(8,128)}, f32[128,128]{1,0...) custom-call(bf16[16,64,128]{2,1,0:T(8,128)(2,1)} %refs_0_.1, bf16[16,64,128]{2,1,0:T(8,128)(2,1)} %refs_1_.1, ...), custom_call_target="tpu_custom_call" | custom-call | tf_op jit(solution)/shard_map/triangle_backward/pallas_call | solution.py:389
  60.2 2.0 %hand_out.1 = (bf16[16,64,128]{2,1,0:T(8,128)(2,1)}, f32[1,128]{1,0:T(1,128)}, f32[1,128]{1,0:T(1,128)}, f32[1,128]{1,0:T(1,128)}, f32[1,128]{1,0:T(1,128)}, /*i...) custom-call(bf16[16,64,128]{2,1,0:T(8,128)(2,1)} %get-tuple-element., ...), custom_call_target="tpu_custom_call" | custom-call | tf_op jit(solution)/shard_map/hand_out/pallas_call | solution.py:416
